TPU v7x, 32 devices: a whole 2x2x4 slice. The times are simulated.
32 devices in a mesh: tok: 8 (over z, x), feat: 4 (over y, core).
Axes of the slice: x: 2, y: 2, z: 4, core: 2. Of those that a mesh axis runs over, the one named last changes fastest.
Arguments:
- train_act: float32 [2048, 16384], P('tok', 'feat'), may hold values from -6 to 6
- train_grad: float32 [2048, 16384], P('tok', 'feat'), may hold values from -6 to 6
- pool_act: float32 [8, 16384], P('tok', 'feat'), may hold values from -6 to 6
- pool_grad: float32 [8, 16384], P('tok', 'feat'), may hold values from -6 to 6
- bite_index: int32 [4, 128], replicated, may hold values from 0 to 7, as said below
Outputs:
- score: float32 [2048], P(('tok', 'feat'))
Inputs may be any that keep to these rules, and one draw needn't show every extreme that they name: `bite_index`: every pool token is named by at least one slot.
All inputs are finite; a program needn't handle non-finite values.
Results may differ from a plain program's by a relative error of at most 0.00017.
Values sent between devices are 32-bit elements; how exact they have to be, the bound alone decides.
No kernel may reach another device: no remote copies, remote signals or barrier semaphores. Data moves between devices by JAX's collectives and lax.ppermute only.
A program may use at most 64 MiB of HBM per device.

v0:
```python
import jax
import jax.numpy as jnp
from jax import lax
from jax.sharding import PartitionSpec as P


def inner_rows(left, right):
    return lax.dot_general(
        left,
        right,
        (((1,), (1,)), ((), ())),
        precision=lax.Precision.HIGHEST,
        preferred_element_type=jnp.float32,
    )


def body(train_act, train_grad, pool_act, pool_grad, bite_index):
    rows, width = train_act.shape
    flat = bite_index.reshape(-1)
    slots = flat.shape[0]
    scale = 1.0 / (width * lax.axis_size("feat") * jnp.sqrt(jnp.float32(slots)))
    whole_act, whole_grad = (
        lax.all_gather(pool_act, "tok", axis=0, tiled=True),
        lax.all_gather(pool_grad, "tok", axis=0, tiled=True),
    )
    val_act = jnp.take(whole_act, flat, axis=0)
    val_grad = jnp.take(whole_grad, flat, axis=0)
    act_part = inner_rows(train_act, val_act)
    grad_part = inner_rows(train_grad, val_grad)
    act_full, grad_full = lax.psum((act_part, grad_part), "feat")
    share = rows // lax.axis_size("feat")
    offset = lax.axis_index("feat") * share
    act_sum = lax.dynamic_slice_in_dim(act_full, offset, share, 0)
    grad_sum = lax.dynamic_slice_in_dim(grad_full, offset, share, 0)
    product = act_sum * grad_sum
    return jnp.sum(product, axis=1) * scale


def solution(mesh):
    return jax.shard_map(
        body,
        mesh=mesh,
        in_specs=(P("tok", "feat"), P("tok", "feat"), P("tok", "feat"), P("tok", "feat"), P()),
        out_specs=P(("tok", "feat")),
        check_vma=False,
    )
```

profile of v0, /device:TPU:0, one launch (start us, length us, event | category | flops | bytes accessed | tf_op | source)
XLA Modules:
  0.0 146.0 jit_solution(169886488539994338)
XLA Ops:
  6.5 0.0 all-reduce.3.cloned.1.call-start
  6.5 0.7 compare_select_fusion
  7.2 0.7 compare_and_fusion
  7.9 32.5 %all-gather.1 = f32[8,1,4096]{2,1,0:T(1,128)S(1)} all-gather(f32[1,1,4096]{2,1,0:T(1,128)} %bitcast.20), channel_id=1, replica_groups=mesh['tok'=8,'feat'=4] {'tok'}, dimensions={0}, use_global_device_ids=true | all-gather | bytes 147456 | tf_op jit(solution)/shard_map/all_gather | solution.py:24
  40.4 0.1 copy.10
  40.5 30.7 %all-gather = f32[8,1,4096]{2,1,0:T(1,128)S(1)} all-gather(f32[1,1,4096]{2,1,0:T(1,128)} %bitcast.21), channel_id=1, replica_groups=mesh['tok'=8,'feat'=4] {'tok'}, dimensions={0}, use_global_device_ids=true | all-gather | bytes 147456 | tf_op jit(solution)/shard_map/all_gather | solution.py:23
  71.3 0.1 copy.11
  71.3 5.1 %gather_fusion.1 = f32[512,4096]{1,0:T(8,128)} fusion(f32[8,4096]{1,0:T(8,128)S(1)} %bitcast.18, s32[1024]{0:T(1024)S(1)} %pad_clamp_fusion), kind=kCustom, calls=%fused_computation.1.clone | custom fusion | bytes 16779264 | tf_op jit(solution)/shard_map/jit(_take)/gather | solution.py:27
  76.5 5.1 %gather_fusion = f32[512,4096]{1,0:T(8,128)} fusion(f32[8,4096]{1,0:T(8,128)S(1)} %bitcast.19, s32[1024]{0:T(1024)S(1)} %pad_clamp_fusion), kind=kCustom, calls=%fused_computation.clone | custom fusion | bytes 16779264 | tf_op jit(solution)/shard_map/jit(_take)/gather | solution.py:26
  81.6 0.0 copy-start
  81.6 0.0 copy-start.1
  81.6 10.8 %fusion.11 = f32[256,512]{0,1:T(8,128)} fusion(f32[256,4096]{1,0:T(8,128)} %param.8, f32[512,4096]{1,0:T(8,128)} %gather_fusion.1, pred[512]{0:T(512)(128)(4,1)S(1)} %compare_and_fusion), kind=kOutput, calls=%fused_computation.11 | convolution fusion | flops 6444548096 | bytes 13107712 | tf_op jit(solution)/shard_map/dot_general | solution.py:8
  92.4 0.0 copy-done
  92.4 0.0 copy-done.1
  92.4 7.7 %fusion.8 = f32[256,512]{0,1:T(8,128)} fusion(f32[256,4096]{1,0:T(8,128)S(1)} %copy-done.1, f32[512,4096]{1,0:T(8,128)S(1)} %copy-done, pred[512]{0:T(512)(128)(4,1)S(1)} %compare_and_fusion), kind=kOutput, calls=%fused_computation.10 | convolution fusion | flops 6444548096 | bytes 13107712 | tf_op jit(solution)/shard_map/dot_general | solution.py:8
  100.1 0.0 all-reduce.3.cloned.1.call-update
  100.1 37.2 %all-reduce.3.cloned.1.call-done = (f32[256,512]{0,1:T(8,128)}, f32[256,512]{0,1:T(8,128)}) async-done(((f32[256,512]{0,1:T(8,128)}, f32[256,512]{0,1:T(8,128)}), (f32[256,512]{0,1:T(8,128)}, f32[256,512]{0,1:T(8,128)})) %all-reduce.3.cloned.1.call-update) | async-done | bytes 1048592 | tf_op jit(solution)/shard_map/psum | solution.py:30
  137.4 1.2 multiply_reduce_fusion
  138.6 0.5 broadcast_multiply_fusion
  (1 shorter events, 0.0 us)
Async XLA Ops:
  6.5 130.8 %all-reduce.3.cloned.1.call-start = ((), (), s32[]{:S(2)}) async-start(), calls=%async_computation | async-start | bytes 2097152 | tf_op jit(solution)/shard_map/psum | solution.py:30
  81.6 10.8 %copy-start = (f32[512,4096]{1,0:T(8,128)S(1)}, f32[512,4096]{1,0:T(8,128)}, u32[]{:S(2)}) copy-start(f32[512,4096]{1,0:T(8,128)} %gather_fusion) | copy-start | bytes 25165828
  81.6 10.8 %copy-start.1 = (f32[256,4096]{1,0:T(8,128)S(1)}, f32[256,4096]{1,0:T(8,128)}, u32[]{:S(2)}) copy-start(f32[256,4096]{1,0:T(8,128)} %param.7) | copy-start | bytes 12582916
Sparse Core Ops, SparseCore 0:
  100.2 37.0 all-reduce.2
where the time goes:
time: 146 us
  blocking collectives  63.2 us (43%)
  waiting for transfers between devices  37.2 us (25%)
  matrix products  18.5 us (13%)
  between operations  13.4 us (9%)
  local copies, waits for them, and re-layouts  10.4 us (7%)
  other arithmetic  3.14 us (2%)
    psum x1, waiting for transfers between devices, body(): act_full, grad_full = lax.psum((act_part, grad_part), 'feat')  37.2 us
    all_gather x1, blocking collectives, body(): lax.all_gather(pool_grad, 'tok', axis=0, tiled=True)  32.5 us
    all_gather x1, blocking collectives, body(): lax.all_gather(pool_act, 'tok', axis=0, tiled=True)  30.7 us
    dot_general x2, matrix products, inner_rows(): lax.dot_general(left, right, (((1,), (1,)), ((), ())), precision=lax.Prec...  18.5 us
    gather x1, local copies, waits for them, and re-layouts, body(): val_grad = jnp.take(whole_grad, flat, axis=0)  5.12 us
    gather x1, local copies, waits for them, and re-layouts, body(): val_act = jnp.take(whole_act, flat, axis=0)  5.1 us
  transfers between devices with their start and end apart: 1, of which 1 were waited for; matrix products, arithmetic and copies ran while one was open for 0% of the time, Pallas kernels for 0%

commit v1 on v0

v1 whole, which is shorter than its diff:
```python
import functools

import jax
import jax.numpy as jnp
from jax import lax
from jax.experimental import pallas as pl
from jax.experimental.pallas import tpu as pltpu
from jax.sharding import PartitionSpec as P

LANES = 128
CHUNKS = 8


def halves(x):
    hi = x.astype(jnp.bfloat16)
    lo = (x - hi.astype(jnp.float32)).astype(jnp.bfloat16)
    return hi, lo


def partner(index, step, size):
    if size & (size - 1) == 0:
        return index ^ step
    return (index + size - step) % size


def factors(n):
    outer = max(d for d in range(1, n + 1) if n % d == 0 and d * d <= n)
    return outer, n // outer


def vmem(*xs):
    return [pltpu.with_memory_space_constraint(x, pltpu.VMEM) for x in xs]


WHOLE = pl.BlockSpec(memory_space=pltpu.VMEM)
SMALL = pltpu.CompilerParams(vmem_limit_bytes=2 << 20)
ANYWHERE = pl.BlockSpec(memory_space=pl.ANY)


def prepare_kernel(act, grad, own, sems):
    block = act.shape[0]
    copies = [pltpu.make_async_copy(src, own.at[pl.ds(i * block, block)], sems.at[i]) for i, src in enumerate((act, grad))]
    for copy in copies:
        copy.start()
    for copy in copies:
        copy.wait()


def prepare(act, grad):
    return pl.pallas_call(
        prepare_kernel,
        out_shape=pltpu.VMEM((2 * act.shape[0], LANES), jnp.float32),
        in_specs=[ANYWHERE, ANYWHERE],
        out_specs=WHOLE,
        scratch_shapes=[pltpu.SemaphoreType.DMA((2,))],
        compiler_params=SMALL,
        name="prepare",
    )(pltpu.with_memory_space_constraint(act, pltpu.HBM), pltpu.with_memory_space_constraint(grad, pltpu.HBM))


def join_kernel(*refs):
    *parts, after, out = refs
    block = parts[0].shape[0]
    for i, part in enumerate(parts):
        out[pl.ds(i * block, block)] = part[...]


def join(parts, after):
    block = parts[0].shape[0]
    return pl.pallas_call(
        join_kernel,
        out_shape=pltpu.VMEM((len(parts) * block, LANES), jnp.float32),
        in_specs=[WHOLE] * len(parts) + [ANYWHERE],
        out_specs=WHOLE,
        compiler_params=SMALL,
        name="join",
    )(*vmem(*parts, after))


def weigh(outer, inner, width, bites, weight):
    n = outer * inner
    me = lax.axis_index("tok")
    row = lax.broadcasted_iota(jnp.int32, (n, LANES), 0)
    token = partner(me // inner, row % outer, outer) * inner + partner(me % inner, row // outer, inner)
    slots = bites.shape[0] * bites.shape[1]
    count = jnp.zeros((n, LANES), jnp.float32)
    for b in range(bites.shape[0]):
        for c in range(bites.shape[1] // LANES):
            count += (bites[b : b + 1, c * LANES : (c + 1) * LANES] == token).astype(jnp.float32)
    total = jnp.sum(count, axis=1, keepdims=True)
    weight[...] = jnp.broadcast_to(total * (1.0 / (width * slots**0.5)), (n, LANES))


def split_rows(train, hi, lo, buf, sems):
    step = train.shape[0] // CHUNKS
    copies = []
    for c in range(CHUNKS):
        copies.append(pltpu.make_async_copy(train.at[pl.ds(c * step, step)], buf.at[c], sems.at[c]))
        copies[c].start()
    for c in range(CHUNKS):
        copies[c].wait()

        @pl.loop(0, step // 16)
        def _(r):
            span = pl.ds(pl.multiple_of(r * 16, 16), 16)
            to = pl.ds(pl.multiple_of(c * step + r * 16, 16), 16)
            hi[to], lo[to] = halves(buf[c, span])


def split_act_kernel(outer, inner, width, train, bites, hi, lo, weight, buf, index, sems, sem):
    copy = pltpu.make_async_copy(bites, index, sem)
    copy.start()
    split_rows(train, hi, lo, buf, sems)
    copy.wait()
    weigh(outer, inner, width, index, weight)


def split_grad_kernel(train, after, hi, lo, buf, sems):
    split_rows(train, hi, lo, buf, sems)


def staging(train):
    return [pltpu.VMEM((CHUNKS, train.shape[0] // CHUNKS, train.shape[1]), jnp.float32)]


def hbm(*xs):
    return [pltpu.with_memory_space_constraint(x, pltpu.HBM) for x in xs]


def split_act(outer, inner, width, train, bites):
    half = pltpu.VMEM(train.shape, jnp.bfloat16)
    return pl.pallas_call(
        functools.partial(split_act_kernel, outer, inner, width),
        out_shape=[half, half, pltpu.VMEM((outer * inner, LANES), jnp.float32)],
        in_specs=[ANYWHERE] * 2,
        out_specs=[WHOLE] * 3,
        scratch_shapes=staging(train)
        + [pltpu.VMEM(bites.shape, jnp.int32), pltpu.SemaphoreType.DMA((CHUNKS,)), pltpu.SemaphoreType.DMA],
        compiler_params=pltpu.CompilerParams(vmem_limit_bytes=6 << 20),
        name="split_act",
    )(*hbm(train, bites))


def split_grad(train, after):
    half = pltpu.VMEM(train.shape, jnp.bfloat16)
    return pl.pallas_call(
        split_grad_kernel,
        out_shape=[half, half],
        in_specs=[ANYWHERE] * 2,
        out_specs=[WHOLE] * 2,
        scratch_shapes=staging(train) + [pltpu.SemaphoreType.DMA((CHUNKS,))],
        compiler_params=pltpu.CompilerParams(vmem_limit_bytes=6 << 20),
        name="split_grad",
    )(*hbm(train), *vmem(after))


def gram_kernel(outer, inner, feat, a_hi, a_lo, g_hi, g_lo, weight, *refs):
    pieces, (own, *sends), (pool,) = refs[:inner], refs[inner : inner + feat], refs[inner + feat :]
    n = outer * inner
    rows, cols = a_hi.shape
    block = pieces[0].shape[0] // outer
    for t in range(inner):
        pool[pl.ds(t * outer * block, outer * block)] = pieces[t][...]
    share = rows // feat
    results = []
    for which, hi, lo in ((0, a_hi, a_lo), (1, g_hi, g_lo)):
        tops, bottoms = [], []
        for q in range(cols // LANES):
            part = pool[pl.ds(which * (block // 2) + q, n, stride=block)]
            top, bottom = halves(part)
            tops.append(top)
            bottoms.append(bottom)
        p_hi = jnp.concatenate(tops, axis=1)
        p_lo = jnp.concatenate(bottoms, axis=1)
        both = jnp.concatenate([p_hi, p_lo], axis=0)
        dims = (((1,), (1,)), ((), ()))
        one = lax.dot_general(both, hi[...], dims, preferred_element_type=jnp.float32)
        two = lax.dot_general(p_hi, lo[...], dims, preferred_element_type=jnp.float32)
        results.append(one[:n] + one[n:] + two)
    act, grad = results
    act = act * jnp.tile(weight[...], (1, rows // LANES))
    me = lax.axis_index("feat")
    for j in range(feat):
        piece = jnp.concatenate([act[:, j * share : (j + 1) * share], grad[:, j * share : (j + 1) * share]], axis=1)
        for s, out in enumerate((own, *sends)):
            to = me ^ s if feat & (feat - 1) == 0 else (me + s) % feat

            @pl.when(to == j)
            def _():
                out[...] = piece


def grams(outer, inner, feat, parts, pieces):
    n = outer * inner
    rows, cols = parts[0].shape
    share = rows // feat
    args = vmem(*parts, *pieces)
    return pl.pallas_call(
        functools.partial(gram_kernel, outer, inner, feat),
        out_shape=[pltpu.VMEM((n, 2 * share), jnp.float32)] * feat,
        in_specs=[WHOLE] * len(args),
        out_specs=[WHOLE] * feat,
        scratch_shapes=[pltpu.VMEM((inner * pieces[0].shape[0], LANES), jnp.float32)],
        compiler_params=pltpu.CompilerParams(vmem_limit_bytes=8 << 20),
        name="grams",
    )(*args)


def finish_kernel(*refs):
    *parts, out = refs
    total = parts[0][...]
    for part in parts[1:]:
        total += part[...]
    share = out.shape[1]
    out[...] = jnp.sum(total[:, :share] * total[:, share:], axis=0, keepdims=True)


def body(train_act, train_grad, pool_act, pool_grad, bites):
    tok, feat = lax.axis_size("tok"), lax.axis_size("feat")
    rows, cols = train_act.shape
    outer, inner = factors(tok)
    own = prepare(pool_act.reshape(-1, LANES), pool_grad.reshape(-1, LANES))

    column = [own]
    for s in range(1, outer):
        pairs = [(partner(i // inner, s, outer) * inner + i % inner, i) for i in range(tok)]
        column.append(lax.ppermute(own, "tok", pairs))
    a_hi, a_lo, weight = split_act(outer, inner, cols * feat, train_act, bites)
    held = join(column, weight)
    pieces = [held]
    for t in range(1, inner):
        pairs = [(i // inner * inner + partner(i % inner, t, inner), i) for i in range(tok)]
        pieces.append(lax.ppermute(held, "tok", pairs))
    g_hi, g_lo = split_grad(train_grad, held)
    parts = a_hi, a_lo, g_hi, g_lo, weight
    mine, *sends = grams(outer, inner, feat, parts, pieces)
    got = [mine]
    for s, send in enumerate(sends, 1):
        pairs = [(i, i ^ s if feat & (feat - 1) == 0 else (i + s) % feat) for i in range(feat)]
        got.append(lax.ppermute(send, "feat", pairs))
    score = pl.pallas_call(
        finish_kernel,
        out_shape=jax.ShapeDtypeStruct((1, rows // feat), jnp.float32),
        in_specs=[WHOLE] * feat,
        out_specs=WHOLE,
        compiler_params=SMALL,
        name="finish",
    )(*vmem(*got))
    return score.reshape(-1)


def solution(mesh):
    return jax.shard_map(
        body,
        mesh=mesh,
        in_specs=(P("tok", "feat"), P("tok", "feat"), P("tok", "feat"), P("tok", "feat"), P()),
        out_specs=P(("tok", "feat")),
        check_vma=False,
    )
```

time: 146 us -> 22.7 us (0.16)
  blocking collectives: 63.2 us -> 0 us
  waiting for transfers between devices: 37.2 us -> 4.11 us
  matrix products: 18.5 us -> 0 us
  between operations: 13.4 us -> 0.05 us
  local copies, waits for them, and re-layouts: 10.4 us -> 0 us
  starting transfers between devices: 0.01 us -> 9.53 us
  Pallas kernels: 0 us -> 8.64 us
  other arithmetic: 3.14 us -> 0 us
    all_gather x2 -> x0, blocking collectives: 63.2 us -> none  [the longest x1 32.5 us: body(): lax.all_gather(pool_grad, 'tok', axis=0, tiled=True)]
    psum x1 -> x0, waiting for transfers between devices: 37.2 us -> none  [body(): act_full, grad_full = lax.psum((act_part, grad_part), 'feat')]
    dot_general x2 -> x0, matrix products: 18.5 us -> none  [inner_rows(): lax.dot_general(left, right, (((1,), (1,)), ((), ())), precision=lax.Prec...]
    gather x2 -> x0, local copies, waits for them, and re-layouts: 10.2 us -> none  [the longest x1 5.12 us: body(): val_grad = jnp.take(whole_grad, flat, axis=0)]
    ppermute x0 -> x7, starting transfers between devices: none -> 9.53 us  [the longest x1 4.1 us: body(): column.append(lax.ppermute(own, 'tok', pairs))]
    pallas_call x0 -> x6, Pallas kernels: none -> 8.64 us  [the longest x1 2.57 us: grams(): pl.pallas_call(functools.partial(gram_kernel, outer, inner, feat), out_sh...]
    ppermute x0 -> x7, waiting for transfers between devices: none -> 4.11 us  [the longest x3 2.69 us: body(): got.append(lax.ppermute(send, 'feat', pairs))]
  transfers between devices with their start and end apart: 1 -> 7, of which waited for: 1 -> 5; matrix products, arithmetic and copies ran while one was open for 0% -> 0% of each run, Pallas kernels for 0% -> 21%
where the time goes in v1:
time: 22.7 us; the launch traced here: 22.3 us
  starting transfers between devices  9.53 us (42%)
  Pallas kernels  8.64 us (38%)
  waiting for transfers between devices  4.11 us (18%)
    ppermute x1, starting transfers between devices, body(): column.append(lax.ppermute(own, 'tok', pairs))  4.1 us
    ppermute x3, starting transfers between devices, body(): pieces.append(lax.ppermute(held, 'tok', pairs))  3.55 us
    ppermute x3, waiting for transfers between devices, body(): got.append(lax.ppermute(send, 'feat', pairs))  2.69 us
    pallas_call x1, Pallas kernels, grams(): pl.pallas_call(functools.partial(gram_kernel, outer, inner, feat), out_sh...  2.57 us
    pallas_call x1, Pallas kernels, split_act(): pl.pallas_call(functools.partial(split_act_kernel, outer, inner, width),...  2.43 us
    pallas_call x1, Pallas kernels, split_grad(): pl.pallas_call(split_grad_kernel, out_shape=[half, half], in_specs=[ANYWH...  2.3 us
    ppermute x3, starting transfers between devices, body(): got.append(lax.ppermute(send, 'feat', pairs))  1.88 us
    ppermute x3, waiting for transfers between devices, body(): pieces.append(lax.ppermute(held, 'tok', pairs))  1.42 us
  transfers between devices with their start and end apart: 7, of which 5 were waited for; matrix products, arithmetic and copies ran while one was open for 0% of the time, Pallas kernels for 21%

profile of v1, /device:TPU:0, one launch (start us, length us, event | category | flops | bytes accessed | tf_op | source)
XLA Modules:
  0.0 22.3 jit_solution(3259298787418418318)
XLA Ops:
  0.0 0.8 %prepare.1.refs_0_ = f32[64,128]{1,0:T(8,128)S(1)} custom-call(f32[32,128]{1,0:T(8,128)} %bitcast.3, f32[32,128]{1,0:T(8,128)} %bitcast.4), custom_call_target="tpu_custom_call" | custom-call | tf_op jit(solution)/shard_map/prepare/pallas_call | solution.py:50
  0.8 4.1 %collective-permute-start = (f32[64,128]{1,0:T(8,128)S(1)}, f32[64,128]{1,0:T(8,128)S(1)}, u32[]{:S(2)}, u32[]{:S(2)}) collective-permute-start(f32[64,128]{1,0:T(8,128)S(1)} %prepare.1.refs_0_), channel_id=1, source_target_pairs={{16,0},{20,4},{24,8},{28,12},{0,16},{4,20},{8,24},{12,28},{17,1},{... | collective-permute-start | bytes 98312 | tf_op jit(solution)/shard_map/ppermute | solution.py:227
  4.9 2.4 %split_act.1 = (bf16[256,4096]{1,0:T(8,128)(2,1)S(1)}, bf16[256,4096]{1,0:T(8,128)(2,1)S(1)}, f32[8,128]{1,0:T(8,128)S(1)}) custom-call(f32[256,4096]{1,0:T(8,128)} %train.2, s32[4,128]{1,0:T(4,128)} %bites.1), custom_call_target="tpu_custom_call" | custom-call | tf_op jit(solution)/shard_map/split_act/pallas_call | solution.py:132
  7.3 0.0 collective-permute-done.refs_1_
  7.3 2.6 %collective-permute-start.3 = (f32[128,128]{1,0:T(8,128)S(1)}, f32[128,128]{1,0:T(8,128)S(1)}, u32[]{:S(2)}, u32[]{:S(2)}) collective-permute-start(f32[128,128]{1,0:T(8,128)S(1)} %join.1.after.refs_0_), channel_id=1, source_target_pairs={{12,0},{8,4},{4,8},{0,12},{28,16},{24,20},{20,24},{16,28},{13,1},{... | collective-permute-start | bytes 196616 | tf_op jit(solution)/shard_map/ppermute | solution.py:233
  9.9 0.4 %collective-permute-start.2 = (f32[128,128]{1,0:T(8,128)S(1)}, f32[128,128]{1,0:T(8,128)S(1)}, u32[]{:S(2)}, u32[]{:S(2)}) collective-permute-start(f32[128,128]{1,0:T(8,128)S(1)} %join.1.after.refs_0_), channel_id=1, source_target_pairs={{8,0},{12,4},{0,8},{4,12},{24,16},{28,20},{16,24},{20,28},{9,1},{1... | collective-permute-start | bytes 196616 | tf_op jit(solution)/shard_map/ppermute | solution.py:233
  10.3 0.5 %collective-permute-start.1 = (f32[128,128]{1,0:T(8,128)S(1)}, f32[128,128]{1,0:T(8,128)S(1)}, u32[]{:S(2)}, u32[]{:S(2)}) collective-permute-start(f32[128,128]{1,0:T(8,128)S(1)} %join.1.after.refs_0_), channel_id=1, source_target_pairs={{4,0},{0,4},{12,8},{8,12},{20,16},{16,20},{28,24},{24,28},{5,1},{1... | collective-permute-start | bytes 196616 | tf_op jit(solution)/shard_map/ppermute | solution.py:233
  10.9 2.3 %split_grad.1 = (bf16[256,4096]{1,0:T(8,128)(2,1)S(1)}, bf16[256,4096]{1,0:T(8,128)(2,1)S(1)}) custom-call(f32[256,4096]{1,0:T(8,128)} %train.3, f32[128,128]{1,0:T(8,128)S(1)} %join.1.after.refs_0_), custom_call_target="tpu_custom_call" | custom-call | tf_op jit(solution)/shard_map/split_grad/pallas_call | solution.py:146
  13.2 0.1 collective-permute-done.3.refs_3_
  13.2 0.9 %collective-permute-done.2.refs_2_ = f32[128,128]{1,0:T(8,128)S(1)} collective-permute-done((f32[128,128]{1,0:T(8,128)S(1)}, f32[128,128]{1,0:T(8,128)S(1)}, u32[]{:S(2)}, u32[]{:S(2)}) %collective-permute-start.2) | collective-permute-done | bytes 65568 | tf_op jit(solution)/shard_map/ppermute | solution.py:233
  14.2 0.4 %collective-permute-done.1.refs_1_ = f32[128,128]{1,0:T(8,128)S(1)} collective-permute-done((f32[128,128]{1,0:T(8,128)S(1)}, f32[128,128]{1,0:T(8,128)S(1)}, u32[]{:S(2)}, u32[]{:S(2)}) %collective-permute-start.1) | collective-permute-done | bytes 65568 | tf_op jit(solution)/shard_map/ppermute | solution.py:233
  14.6 2.6 %grams.1 = (f32[8,128]{1,0:T(8,128)S(1)}, f32[8,128]{1,0:T(8,128)S(1)}, f32[8,128]{1,0:T(8,128)S(1)}, f32[8,128]{1,0:T(8,128)S(1)}) custom-call(bf16[256,4096]{1,0:T(8,128)(2,1)S(1)} %get-tuple-element.14.a_hi, bf16[256,4096]{1,0:T(8,128)(2,1)S(1)} %get-tuple-element.15.a_lo, bf16[256,4096]{1,0:T(8,128)(2,1)S(1)} %get-tuple-element.17.g_hi, ...), custom_call_target="tpu_custom_call" | custom-call | tf_op jit(solution)/shard_map/grams/pallas_call | solution.py:198
  17.2 0.0 collective-permute-start.4
  17.2 1.5 %collective-permute-start.5 = (f32[8,128]{1,0:T(8,128)S(1)}, f32[8,128]{1,0:T(8,128)S(1)}, u32[]{:S(2)}, u32[]{:S(2)}) collective-permute-start(f32[8,128]{1,0:T(8,128)S(1)} %get-tuple-element.21), channel_id=1, source_target_pairs={{0,2},{1,3},{2,0},{3,1},{4,6},{5,7},{6,4},{7,5},{8,10},{9,11},{10,... | collective-permute-start | bytes 12296 | tf_op jit(solution)/shard_map/ppermute | solution.py:240
  18.7 0.3 %collective-permute-start.6 = (f32[8,128]{1,0:T(8,128)S(1)}, f32[8,128]{1,0:T(8,128)S(1)}, u32[]{:S(2)}, u32[]{:S(2)}) collective-permute-start(f32[8,128]{1,0:T(8,128)S(1)} %get-tuple-element.22), channel_id=1, source_target_pairs={{0,3},{1,2},{2,1},{3,0},{4,7},{5,6},{6,5},{7,4},{8,11},{9,10},{10,... | collective-permute-start | bytes 12296 | tf_op jit(solution)/shard_map/ppermute | solution.py:240
  19.1 0.0 collective-permute-done.4.refs_1_
  19.1 1.7 %collective-permute-done.5.refs_2_ = f32[8,128]{1,0:T(8,128)S(1)} collective-permute-done((f32[8,128]{1,0:T(8,128)S(1)}, f32[8,128]{1,0:T(8,128)S(1)}, u32[]{:S(2)}, u32[]{:S(2)}) %collective-permute-start.5) | collective-permute-done | bytes 4128 | tf_op jit(solution)/shard_map/ppermute | solution.py:240
  20.8 0.9 %collective-permute-done.6.refs_3_ = f32[8,128]{1,0:T(8,128)S(1)} collective-permute-done((f32[8,128]{1,0:T(8,128)S(1)}, f32[8,128]{1,0:T(8,128)S(1)}, u32[]{:S(2)}, u32[]{:S(2)}) %collective-permute-start.6) | collective-permute-done | bytes 4128 | tf_op jit(solution)/shard_map/ppermute | solution.py:240
  21.8 0.6 %finish.1 = f32[1,64]{1,0:T(1,128)} custom-call(f32[8,128]{1,0:T(8,128)S(1)} %get-tuple-element.19.refs_0_, f32[8,128]{1,0:T(8,128)S(1)} %collective-permute-done.4.refs_1_, f32[8,128]{1,0:T(8,128)S(1)} %collective-permute-done.5.refs_2_, f32[8,128]{1,0:T(8,128)S(1)} %collective-permute-done.6.refs_3_), custom_call_target="tpu_custom_call" | custom-call | tf_op jit(solution)/shard_map/finish/pallas_call | solution.py:241
  (1 shorter events, 0.0 us)
Async XLA Ops:
  0.8 6.5 %collective-permute-start = (f32[64,128]{1,0:T(8,128)S(1)}, f32[64,128]{1,0:T(8,128)S(1)}, u32[]{:S(2)}, u32[]{:S(2)}) collective-permute-start(f32[64,128]{1,0:T(8,128)S(1)} %prepare.1.refs_0_), channel_id=1, source_target_pairs={{16,0},{20,4},{24,8},{28,12},{0,16},{4,20},{8,24},{12,28},{17,1},{... | collective-permute-start | bytes 98312 | tf_op jit(solution)/shard_map/ppermute | solution.py:227
  7.3 5.9 %collective-permute-start.3 = (f32[128,128]{1,0:T(8,128)S(1)}, f32[128,128]{1,0:T(8,128)S(1)}, u32[]{:S(2)}, u32[]{:S(2)}) collective-permute-start(f32[128,128]{1,0:T(8,128)S(1)} %join.1.after.refs_0_), channel_id=1, source_target_pairs={{12,0},{8,4},{4,8},{0,12},{28,16},{24,20},{20,24},{16,28},{13,1},{... | collective-permute-start | bytes 196616 | tf_op jit(solution)/shard_map/ppermute | solution.py:233
  9.9 4.3 %collective-permute-start.2 = (f32[128,128]{1,0:T(8,128)S(1)}, f32[128,128]{1,0:T(8,128)S(1)}, u32[]{:S(2)}, u32[]{:S(2)}) collective-permute-start(f32[128,128]{1,0:T(8,128)S(1)} %join.1.after.refs_0_), channel_id=1, source_target_pairs={{8,0},{12,4},{0,8},{4,12},{24,16},{28,20},{16,24},{20,28},{9,1},{1... | collective-permute-start | bytes 196616 | tf_op jit(solution)/shard_map/ppermute | solution.py:233
  10.3 4.3 %collective-permute-start.1 = (f32[128,128]{1,0:T(8,128)S(1)}, f32[128,128]{1,0:T(8,128)S(1)}, u32[]{:S(2)}, u32[]{:S(2)}) collective-permute-start(f32[128,128]{1,0:T(8,128)S(1)} %join.1.after.refs_0_), channel_id=1, source_target_pairs={{4,0},{0,4},{12,8},{8,12},{20,16},{16,20},{28,24},{24,28},{5,1},{1... | collective-permute-start | bytes 196616 | tf_op jit(solution)/shard_map/ppermute | solution.py:233
  17.2 1.9 %collective-permute-start.4 = (f32[8,128]{1,0:T(8,128)S(1)}, f32[8,128]{1,0:T(8,128)S(1)}, u32[]{:S(2)}, u32[]{:S(2)}) collective-permute-start(f32[8,128]{1,0:T(8,128)S(1)} %get-tuple-element.20), channel_id=1, source_target_pairs={{0,1},{1,0},{2,3},{3,2},{4,5},{5,4},{6,7},{7,6},{8,9},{9,8},{10,11... | collective-permute-start | bytes 12296 | tf_op jit(solution)/shard_map/ppermute | solution.py:240
  17.2 3.6 %collective-permute-start.5 = (f32[8,128]{1,0:T(8,128)S(1)}, f32[8,128]{1,0:T(8,128)S(1)}, u32[]{:S(2)}, u32[]{:S(2)}) collective-permute-start(f32[8,128]{1,0:T(8,128)S(1)} %get-tuple-element.21), channel_id=1, source_target_pairs={{0,2},{1,3},{2,0},{3,1},{4,6},{5,7},{6,4},{7,5},{8,10},{9,11},{10,... | collective-permute-start | bytes 12296 | tf_op jit(solution)/shard_map/ppermute | solution.py:240
  18.7 3.0 %collective-permute-start.6 = (f32[8,128]{1,0:T(8,128)S(1)}, f32[8,128]{1,0:T(8,128)S(1)}, u32[]{:S(2)}, u32[]{:S(2)}) collective-permute-start(f32[8,128]{1,0:T(8,128)S(1)} %get-tuple-element.22), channel_id=1, source_target_pairs={{0,3},{1,2},{2,1},{3,0},{4,7},{5,6},{6,5},{7,4},{8,11},{9,10},{10,... | collective-permute-start | bytes 12296 | tf_op jit(solution)/shard_map/ppermute | solution.py:240

commit v2 on v1

v2 whole, which is shorter than its diff:
```python
import functools

import jax
import jax.numpy as jnp
from jax import lax
from jax.experimental import pallas as pl
from jax.experimental.pallas import tpu as pltpu
from jax.sharding import PartitionSpec as P

LANES = 128
CORES = 2


def halves(x):
    hi = x.astype(jnp.bfloat16)
    lo = (x - hi.astype(jnp.float32)).astype(jnp.bfloat16)
    return hi, lo


def partner(index, step, size):
    if size & (size - 1) == 0:
        return index ^ step
    return (index + size - step) % size


def partner_to(index, step, size):
    if size & (size - 1) == 0:
        return index ^ step
    return (index + step) % size


def factors(n):
    outer = max(d for d in range(1, n + 1) if n % d == 0 and d * d <= n)
    return outer, n // outer


def vmem(*xs):
    return [pltpu.with_memory_space_constraint(x, pltpu.VMEM) for x in xs]


WHOLE = pl.BlockSpec(memory_space=pltpu.VMEM)
SMALL = pltpu.CompilerParams(vmem_limit_bytes=2 << 20)
ANYWHERE = pl.BlockSpec(memory_space=pl.ANY)


def prepare_kernel(act, grad, own, sems):
    block = act.shape[0]
    copies = [pltpu.make_async_copy(src, own.at[pl.ds(i * block, block)], sems.at[i]) for i, src in enumerate((act, grad))]
    for copy in copies:
        copy.start()
    for copy in copies:
        copy.wait()


def prepare(act, grad):
    return pl.pallas_call(
        prepare_kernel,
        out_shape=pltpu.VMEM((2 * act.shape[0], LANES), jnp.float32),
        in_specs=[ANYWHERE, ANYWHERE],
        out_specs=WHOLE,
        scratch_shapes=[pltpu.SemaphoreType.DMA((2,))],
        compiler_params=SMALL,
        name="prepare",
    )(pltpu.with_memory_space_constraint(act, pltpu.HBM), pltpu.with_memory_space_constraint(grad, pltpu.HBM))


def stage_kernel(own, train_act, train_grad, out):
    out[...] = own[...]


def stage(own, *trains):
    return pl.pallas_call(
        stage_kernel,
        out_shape=pltpu.VMEM(own.shape, jnp.float32),
        in_specs=[WHOLE, ANYWHERE, ANYWHERE],
        out_specs=WHOLE,
        compiler_params=SMALL,
        name="stage",
    )(*vmem(own), *[pltpu.with_memory_space_constraint(x, pltpu.HBM) for x in trains])


def join_kernel(*refs):
    *parts, out = refs
    block = parts[0].shape[0]
    for i, part in enumerate(parts):
        out[pl.ds(i * block, block)] = part[...]


def join(parts):
    block = parts[0].shape[0]
    return pl.pallas_call(
        join_kernel,
        out_shape=pltpu.VMEM((len(parts) * block, LANES), jnp.float32),
        in_specs=[WHOLE] * len(parts),
        out_specs=WHOLE,
        compiler_params=SMALL,
        name="join",
    )(*vmem(*parts))


def weigh(outer, inner, width, bites, weight):
    n = outer * inner
    me = lax.axis_index("tok")
    row = lax.broadcasted_iota(jnp.int32, (n, LANES), 0)
    token = partner(me // inner, row % outer, outer) * inner + partner(me % inner, row // outer, inner)
    slots = bites.shape[0] * bites.shape[1]
    count = jnp.zeros((n, LANES), jnp.float32)
    for b in range(bites.shape[0]):
        for c in range(bites.shape[1] // LANES):
            count += (bites[b : b + 1, c * LANES : (c + 1) * LANES] == token).astype(jnp.float32)
    total = jnp.sum(count, axis=1, keepdims=True)
    weight[...] = jnp.broadcast_to(total * (1.0 / (width * slots**0.5)), (n, LANES))


def split_rows(train, hi, lo):
    @pl.loop(0, train.shape[0] // 16)
    def _(r):
        span = pl.ds(pl.multiple_of(r * 16, 16), 16)
        hi[span], lo[span] = halves(train[span])


def split_kernel(outer, inner, width, act, grad, bites, after, a_hi, a_lo, g_hi, g_lo, weight, index, sem):
    copy = pltpu.make_async_copy(bites, index, sem)
    copy.start()
    split_rows(act, a_hi, a_lo)
    split_rows(grad, g_hi, g_lo)
    copy.wait()
    weigh(outer, inner, width, index, weight)


def split(outer, inner, width, act, grad, bites, after):
    half = pltpu.VMEM(act.shape, jnp.bfloat16)
    return pl.pallas_call(
        functools.partial(split_kernel, outer, inner, width),
        out_shape=[half] * 4 + [pltpu.VMEM((outer * inner, LANES), jnp.float32)],
        in_specs=[WHOLE, WHOLE, ANYWHERE, ANYWHERE],
        out_specs=[WHOLE] * 5,
        scratch_shapes=[pltpu.VMEM(bites.shape, jnp.int32), pltpu.SemaphoreType.DMA],
        compiler_params=SMALL,
        name="split",
    )(*vmem(act, grad), pltpu.with_memory_space_constraint(bites, pltpu.HBM), *vmem(after))


def rows_of(pool, which, n, cols, block):
    tops, bottoms = [], []
    for q in range(cols // LANES):
        top, bottom = halves(pool[pl.ds(which * (block // 2) + q, n, stride=block)])
        tops.append(top)
        bottoms.append(bottom)
    return jnp.concatenate([jnp.concatenate(tops, axis=1), jnp.concatenate(bottoms, axis=1)], axis=0)


def product(both, hi, lo, start, rows):
    n = both.shape[0] // 2
    dims = (((1,), (1,)), ((), ()))
    span = pl.ds(pl.multiple_of(start, 32), rows)
    one = lax.dot_general(both, hi[span], dims, preferred_element_type=jnp.float32)
    two = lax.dot_general(both[:n], lo[span], dims, preferred_element_type=jnp.float32)
    return one[:n] + one[n:] + two


def device_grams(act_pool, grad_pool, parts, weight, to, share):
    a_hi, a_lo, g_hi, g_lo = parts
    act = product(act_pool[...], a_hi, a_lo, to * share, share) * weight[:, :share]
    grad = product(grad_pool[...], g_hi, g_lo, to * share, share)
    return jnp.concatenate([act, grad], axis=1)


def chip_grams(act_pool, grad_pool, parts, weight, chip, share):
    a_hi, a_lo, g_hi, g_lo = parts
    rows = CORES * share
    act = product(act_pool[...], a_hi, a_lo, chip * rows, rows) * weight[:, :rows]
    grad = product(grad_pool[...], g_hi, g_lo, chip * rows, rows)
    return [
        jnp.concatenate([act[:, c * share : (c + 1) * share], grad[:, c * share : (c + 1) * share]], axis=1)
        for c in range(CORES)
    ]


def swap(pieces, me, mine, other):
    mine[...] = jnp.where(me % CORES == 0, pieces[0], pieces[1])
    other[...] = jnp.where(me % CORES == 0, pieces[1], pieces[0])


def far_kernel(outer, inner, feat, a_hi, a_lo, g_hi, g_lo, weight, *refs):
    pieces, (act_pool, grad_pool, *outs), (pool,) = refs[:inner], refs[inner:-1], refs[-1:]
    n = outer * inner
    rows, cols = a_hi.shape
    block = pieces[0].shape[0] // outer
    start = 0
    for piece in pieces:
        pool[pl.ds(start, piece.shape[0])] = piece[...]
        start += piece.shape[0]
    act_pool[...] = rows_of(pool, 0, n, cols, block)
    grad_pool[...] = rows_of(pool, 1, n, cols, block)
    me = lax.axis_index("feat")
    chips = feat // CORES
    for s in range(1, chips):
        to = partner_to(me // CORES, s, chips)
        got = chip_grams(act_pool, grad_pool, (a_hi, a_lo, g_hi, g_lo), weight, to, rows // feat)
        swap(got, me, outs[CORES * (s - 1)], outs[CORES * (s - 1) + 1])


def near_kernel(feat, step, a_hi, a_lo, g_hi, g_lo, weight, act_pool, grad_pool, after, out):
    me = lax.axis_index("feat")
    to = me // CORES * CORES + (me + step) % CORES
    out[...] = device_grams(act_pool, grad_pool, (a_hi, a_lo, g_hi, g_lo), weight, to, a_hi.shape[0] // feat)


def far(outer, inner, feat, parts, pieces):
    n = outer * inner
    rows, cols = parts[0].shape
    args = vmem(*parts, *pieces)
    piece = pltpu.VMEM((n, 2 * rows // feat), jnp.float32)
    outs = [pltpu.VMEM((2 * n, cols), jnp.bfloat16)] * 2 + [piece] * (feat - CORES)
    return pl.pallas_call(
        functools.partial(far_kernel, outer, inner, feat),
        out_shape=outs,
        in_specs=[WHOLE] * len(args),
        out_specs=[WHOLE] * len(outs),
        scratch_shapes=[pltpu.VMEM((inner * pieces[0].shape[0], LANES), jnp.float32)],
        compiler_params=pltpu.CompilerParams(vmem_limit_bytes=8 << 20),
        name="far",
    )(*args)


def near(feat, step, parts, pools, after):
    args = vmem(*parts, *pools, after)
    return pl.pallas_call(
        functools.partial(near_kernel, feat, step),
        out_shape=pltpu.VMEM((pools[0].shape[0] // 2, 2 * parts[0].shape[0] // feat), jnp.float32),
        in_specs=[WHOLE] * (len(args) - 1) + [ANYWHERE],
        out_specs=WHOLE,
        compiler_params=pltpu.CompilerParams(vmem_limit_bytes=8 << 20),
        name="near",
    )(*args)


def add_kernel(*refs):
    *parts, out = refs
    total = parts[0][...]
    for part in parts[1:]:
        total += part[...]
    out[...] = total


def tally(parts):
    return pl.pallas_call(
        add_kernel,
        out_shape=pltpu.VMEM(parts[0].shape, jnp.float32),
        in_specs=[WHOLE] * len(parts),
        out_specs=WHOLE,
        compiler_params=SMALL,
        name="add",
    )(*vmem(*parts))


def finish_kernel(*refs):
    *parts, out = refs
    total = parts[0][...]
    for part in parts[1:]:
        total += part[...]
    share = out.shape[1]
    out[...] = jnp.sum(total[:, :share] * total[:, share:], axis=0, keepdims=True)


def body(train_act, train_grad, pool_act, pool_grad, bites):
    tok, feat = lax.axis_size("tok"), lax.axis_size("feat")
    rows, cols = train_act.shape
    outer, inner = factors(tok)
    own = prepare(pool_act.reshape(-1, LANES), pool_grad.reshape(-1, LANES))

    own = stage(own, train_act, train_grad)
    across = [[(partner(i // inner, s, outer) * inner + i % inner, i) for i in range(tok)] for s in range(1, outer)]
    along = [[(i // inner * inner + partner(i % inner, t, inner), i) for i in range(tok)] for t in range(1, inner)]
    held = join([own] + [lax.ppermute(own, "tok", pairs) for pairs in across])
    pieces = [held] + [lax.ppermute(held, "tok", pairs) for pairs in along]
    parts = split(outer, inner, cols * feat, train_act, train_grad, bites, held)
    act_pool, grad_pool, *sends = far(outer, inner, feat, parts, pieces)
    chips = feat // CORES
    got = []
    for s, send in enumerate(sends, CORES):
        pairs = [(i, partner_to(i // CORES, s // CORES, chips) * CORES + (i + s) % CORES) for i in range(feat)]
        got.append(lax.ppermute(send, "feat", pairs))
    other = near(feat, 1, parts, (act_pool, grad_pool), sends[0])
    beside = lax.ppermute(other, "feat", [(i, i // CORES * CORES + (i + 1) % CORES) for i in range(feat)])
    got = [tally([*got, near(feat, 0, parts, (act_pool, grad_pool), other)]), beside]
    score = pl.pallas_call(
        finish_kernel,
        out_shape=jax.ShapeDtypeStruct((1, rows // feat), jnp.float32),
        in_specs=[WHOLE] * len(got),
        out_specs=WHOLE,
        compiler_params=SMALL,
        name="finish",
    )(*vmem(*got))
    return score.reshape(-1)


def solution(mesh):
    return jax.shard_map(
        body,
        mesh=mesh,
        in_specs=(P("tok", "feat"), P("tok", "feat"), P("tok", "feat"), P("tok", "feat"), P()),
        out_specs=P(("tok", "feat")),
        check_vma=False,
    )
```

time: 22.7 us -> 20.5 us (0.903)
  Pallas kernels: 8.64 us -> 5.69 us
  waiting for transfers between devices: 4.11 us -> 4.92 us
    ppermute x4 -> x5, waiting for transfers between devices: 1.42 us -> 4.58 us  [the longest x3 2.34 us: body(): pieces = [held] + [lax.ppermute(held, 'tok', pairs) for pairs in along]]
    pallas_call x3 -> x6, Pallas kernels: 7.3 us -> 4.34 us  [the longest x1 1.59 us: split(): pl.pallas_call(functools.partial(split_kernel, outer, inner, width), out_...]
    ppermute x3 -> x2, waiting for transfers between devices: 2.69 us -> 0.33 us  [body(): got.append(lax.ppermute(send, 'feat', pairs))]
    ppermute x3 -> x2, starting transfers between devices: 1.88 us -> 1.58 us  [body(): got.append(lax.ppermute(send, 'feat', pairs))]
    ppermute x4 -> x5, starting transfers between devices: 7.66 us -> 7.91 us  [the longest x1 4.1 us: body(): held = join([own] + [lax.ppermute(own, 'tok', pairs) for pairs in across])]
  transfers between devices with their start and end apart: 7 -> 7, of which waited for: 5 -> 5; matrix products, arithmetic and copies ran while one was open for 0% -> 0% of each run, Pallas kernels for 21% -> 15%
where the time goes in v2:
time: 20.5 us; the launch traced here: 20.2 us
  starting transfers between devices  9.5 us (46%)
  Pallas kernels  5.69 us (28%)
  waiting for transfers between devices  4.92 us (24%)
    ppermute x1, starting transfers between devices, body(): held = join([own] + [lax.ppermute(own, 'tok', pairs) for pairs in across])  4.1 us
    ppermute x3, starting transfers between devices, body(): pieces = [held] + [lax.ppermute(held, 'tok', pairs) for pairs in along]  3.49 us
    ppermute x3, waiting for transfers between devices, body(): pieces = [held] + [lax.ppermute(held, 'tok', pairs) for pairs in along]  2.34 us
    ppermute x1, waiting for transfers between devices, body(): held = join([own] + [lax.ppermute(own, 'tok', pairs) for pairs in across])  2.25 us
    pallas_call x1, Pallas kernels, split(): pl.pallas_call(functools.partial(split_kernel, outer, inner, width), out_...  1.59 us
    ppermute x2, starting transfers between devices, body(): got.append(lax.ppermute(send, 'feat', pairs))  1.58 us
    pallas_call x2, Pallas kernels, near(): pl.pallas_call(functools.partial(near_kernel, feat, step), out_shape=pltp...  1.43 us
    pallas_call x1, Pallas kernels, far(): pl.pallas_call(functools.partial(far_kernel, outer, inner, feat), out_sha...  1.32 us
  transfers between devices with their start and end apart: 7, of which 5 were waited for; matrix products, arithmetic and copies ran while one was open for 0% of the time, Pallas kernels for 15%

profile of v2, /device:TPU:0, one launch (start us, length us, event | category | flops | bytes accessed | tf_op | source)
XLA Modules:
  0.0 20.2 jit_solution(11830995472197937672)
XLA Ops:
  0.0 0.8 %prepare.1.own = f32[64,128]{1,0:T(8,128)S(1)} custom-call(f32[32,128]{1,0:T(8,128)} %bitcast.3, f32[32,128]{1,0:T(8,128)} %bitcast.4), custom_call_target="tpu_custom_call" | custom-call | tf_op jit(solution)/shard_map/prepare/pallas_call | solution.py:56
  0.8 0.0 copy-start
  0.8 0.0 copy-start.1
  0.8 4.1 %collective-permute-start = (f32[64,128]{1,0:T(8,128)S(1)}, f32[64,128]{1,0:T(8,128)S(1)}, u32[]{:S(2)}, u32[]{:S(2)}) collective-permute-start(f32[64,128]{1,0:T(8,128)S(1)} %stage.1.refs_0_), channel_id=1, source_target_pairs={{16,0},{20,4},{24,8},{28,12},{0,16},{4,20},{8,24},{12,28},{17,1},{... | collective-permute-start | bytes 98312 | tf_op jit(solution)/shard_map/ppermute | solution.py:276
  4.9 2.2 %collective-permute-done.refs_1_ = f32[64,128]{1,0:T(8,128)S(1)} collective-permute-done((f32[64,128]{1,0:T(8,128)S(1)}, f32[64,128]{1,0:T(8,128)S(1)}, u32[]{:S(2)}, u32[]{:S(2)}) %collective-permute-start) | collective-permute-done | bytes 32800 | tf_op jit(solution)/shard_map/ppermute | solution.py:276
  7.1 2.5 %collective-permute-start.3 = (f32[128,128]{1,0:T(8,128)S(1)}, f32[128,128]{1,0:T(8,128)S(1)}, u32[]{:S(2)}, u32[]{:S(2)}) collective-permute-start(f32[128,128]{1,0:T(8,128)S(1)} %join.1.after.refs_0_), channel_id=1, source_target_pairs={{12,0},{8,4},{4,8},{0,12},{28,16},{24,20},{20,24},{16,28},{13,1},{... | collective-permute-start | bytes 196616 | tf_op jit(solution)/shard_map/ppermute | solution.py:277
  9.6 0.7 %collective-permute-start.2 = (f32[128,128]{1,0:T(8,128)S(1)}, f32[128,128]{1,0:T(8,128)S(1)}, u32[]{:S(2)}, u32[]{:S(2)}) collective-permute-start(f32[128,128]{1,0:T(8,128)S(1)} %join.1.after.refs_0_), channel_id=1, source_target_pairs={{8,0},{12,4},{0,8},{4,12},{24,16},{28,20},{16,24},{20,28},{9,1},{1... | collective-permute-start | bytes 196616 | tf_op jit(solution)/shard_map/ppermute | solution.py:277
  10.3 0.3 %collective-permute-start.1 = (f32[128,128]{1,0:T(8,128)S(1)}, f32[128,128]{1,0:T(8,128)S(1)}, u32[]{:S(2)}, u32[]{:S(2)}) collective-permute-start(f32[128,128]{1,0:T(8,128)S(1)} %join.1.after.refs_0_), channel_id=1, source_target_pairs={{4,0},{0,4},{12,8},{8,12},{20,16},{16,20},{28,24},{24,28},{5,1},{1... | collective-permute-start | bytes 196616 | tf_op jit(solution)/shard_map/ppermute | solution.py:277
  10.6 0.0 copy-done
  10.6 0.0 copy-done.1
  10.6 1.6 %split.1 = (bf16[256,4096]{1,0:T(8,128)(2,1)S(1)}, bf16[256,4096]{1,0:T(8,128)(2,1)S(1)}, bf16[256,4096]{1,0:T(8,128)(2,1)S(1)}, bf16[256,4096]{1,0:T(8,128)(2,1)S(1)}, f32[8,128]{1,0:T(8,128)S(1)}) custom-call(f32[256,4096]{1,0:T(8,128)S(1)} %copy-done, f32[256,4096]{1,0:T(8,128)S(1)} %copy-done.1, s32[4,128]{1,0:T(4,128)} %bites.1, ...), custom_call_target="tpu_custom_call" | custom-call | tf_op jit(solution)/shard_map/split/pallas_call | solution.py:133
  12.2 0.1 collective-permute-done.3.refs_3_
  12.3 1.6 %collective-permute-done.2.refs_2_ = f32[128,128]{1,0:T(8,128)S(1)} collective-permute-done((f32[128,128]{1,0:T(8,128)S(1)}, f32[128,128]{1,0:T(8,128)S(1)}, u32[]{:S(2)}, u32[]{:S(2)}) %collective-permute-start.2) | collective-permute-done | bytes 65568 | tf_op jit(solution)/shard_map/ppermute | solution.py:277
  13.9 0.7 %collective-permute-done.1.refs_1_ = f32[128,128]{1,0:T(8,128)S(1)} collective-permute-done((f32[128,128]{1,0:T(8,128)S(1)}, f32[128,128]{1,0:T(8,128)S(1)}, u32[]{:S(2)}, u32[]{:S(2)}) %collective-permute-start.1) | collective-permute-done | bytes 65568 | tf_op jit(solution)/shard_map/ppermute | solution.py:277
  14.6 1.3 %far.1 = (bf16[16,4096]{1,0:T(8,128)(2,1)S(1)}, bf16[16,4096]{1,0:T(8,128)(2,1)S(1)}, f32[8,128]{1,0:T(8,128)S(1)}, f32[8,128]{1,0:T(8,128)S(1)}) custom-call(bf16[256,4096]{1,0:T(8,128)(2,1)S(1)} %get-tuple-element.14.a_hi, bf16[256,4096]{1,0:T(8,128)(2,1)S(1)} %get-tuple-element.15.a_lo, bf16[256,4096]{1,0:T(8,128)(2,1)S(1)} %get-tuple-element.16.g_hi, ...), custom_call_target="tpu_custom_call" | custom-call | tf_op jit(solution)/shard_map/far/pallas_call | solution.py:216
  15.9 0.0 collective-permute-start.5
  15.9 1.6 %collective-permute-start.4 = (f32[8,128]{1,0:T(8,128)S(1)}, f32[8,128]{1,0:T(8,128)S(1)}, u32[]{:S(2)}, u32[]{:S(2)}) collective-permute-start(f32[8,128]{1,0:T(8,128)S(1)} %get-tuple-element.19.after), channel_id=1, source_target_pairs={{0,2},{1,3},{2,0},{3,1},{4,6},{5,7},{6,4},{7,5},{8,10},{9,11},{10,... | collective-permute-start | bytes 12296 | tf_op jit(solution)/shard_map/ppermute | solution.py:284
  17.5 0.7 %near.2.after = f32[8,128]{1,0:T(8,128)S(1)} custom-call(bf16[256,4096]{1,0:T(8,128)(2,1)S(1)} %get-tuple-element.14.a_hi, bf16[256,4096]{1,0:T(8,128)(2,1)S(1)} %get-tuple-element.15.a_lo, bf16[256,4096]{1,0:T(8,128)(2,1)S(1)} %get-tuple-element.16.g_hi, bf16[256,4096]{1,0:T(8,128)(2,1)S(1)} %get-tuple-element.17.g_lo, ...), custom_call_target="tpu_custom_call" | custom-call | tf_op jit(solution)/shard_map/near/pallas_call | solution.py:229
  18.2 0.3 %collective-permute-start.6 = (f32[8,128]{1,0:T(8,128)S(1)}, f32[8,128]{1,0:T(8,128)S(1)}, u32[]{:S(2)}, u32[]{:S(2)}) collective-permute-start(f32[8,128]{1,0:T(8,128)S(1)} %near.2.after), channel_id=1, source_target_pairs={{0,1},{1,0},{2,3},{3,2},{4,5},{5,4},{6,7},{7,6},{8,9},{9,8},{10,11... | collective-permute-start | bytes 12296 | tf_op jit(solution)/shard_map/ppermute | solution.py:286
  18.5 0.7 %near.3.refs_2_ = f32[8,128]{1,0:T(8,128)S(1)} custom-call(bf16[256,4096]{1,0:T(8,128)(2,1)S(1)} %get-tuple-element.14.a_hi, bf16[256,4096]{1,0:T(8,128)(2,1)S(1)} %get-tuple-element.15.a_lo, bf16[256,4096]{1,0:T(8,128)(2,1)S(1)} %get-tuple-element.16.g_hi, bf16[256,4096]{1,0:T(8,128)(2,1)S(1)} %get-tuple-element.17.g_lo, ...), custom_call_target="tpu_custom_call" | custom-call | tf_op jit(solution)/shard_map/near/pallas_call | solution.py:229
  19.2 0.0 collective-permute-done.5.refs_1_
  19.2 0.3 %collective-permute-done.4.refs_0_ = f32[8,128]{1,0:T(8,128)S(1)} collective-permute-done((f32[8,128]{1,0:T(8,128)S(1)}, f32[8,128]{1,0:T(8,128)S(1)}, u32[]{:S(2)}, u32[]{:S(2)}) %collective-permute-start.4) | collective-permute-done | bytes 4128 | tf_op jit(solution)/shard_map/ppermute | solution.py:284
  19.6 0.0 collective-permute-done.6.refs_1_
  19.6 0.6 %finish.1 = f32[1,64]{1,0:T(1,128)} custom-call(f32[8,128]{1,0:T(8,128)S(1)} %add.1.refs_0_, f32[8,128]{1,0:T(8,128)S(1)} %collective-permute-done.6.refs_1_), custom_call_target="tpu_custom_call" | custom-call | tf_op jit(solution)/shard_map/finish/pallas_call | solution.py:288
  (3 shorter events, 0.0 us)
Async XLA Ops:
  0.8 9.9 %copy-start = (f32[256,4096]{1,0:T(8,128)S(1)}, f32[256,4096]{1,0:T(8,128)}, u32[]{:S(2)}) copy-start(f32[256,4096]{1,0:T(8,128)} %act.1) | copy-start | bytes 12582916
  0.8 9.9 %copy-start.1 = (f32[256,4096]{1,0:T(8,128)S(1)}, f32[256,4096]{1,0:T(8,128)}, u32[]{:S(2)}) copy-start(f32[256,4096]{1,0:T(8,128)} %grad.1) | copy-start | bytes 12582916
  0.8 6.3 %collective-permute-start = (f32[64,128]{1,0:T(8,128)S(1)}, f32[64,128]{1,0:T(8,128)S(1)}, u32[]{:S(2)}, u32[]{:S(2)}) collective-permute-start(f32[64,128]{1,0:T(8,128)S(1)} %stage.1.refs_0_), channel_id=1, source_target_pairs={{16,0},{20,4},{24,8},{28,12},{0,16},{4,20},{8,24},{12,28},{17,1},{... | collective-permute-start | bytes 98312 | tf_op jit(solution)/shard_map/ppermute | solution.py:276
  7.1 5.2 %collective-permute-start.3 = (f32[128,128]{1,0:T(8,128)S(1)}, f32[128,128]{1,0:T(8,128)S(1)}, u32[]{:S(2)}, u32[]{:S(2)}) collective-permute-start(f32[128,128]{1,0:T(8,128)S(1)} %join.1.after.refs_0_), channel_id=1, source_target_pairs={{12,0},{8,4},{4,8},{0,12},{28,16},{24,20},{20,24},{16,28},{13,1},{... | collective-permute-start | bytes 196616 | tf_op jit(solution)/shard_map/ppermute | solution.py:277
  9.6 4.3 %collective-permute-start.2 = (f32[128,128]{1,0:T(8,128)S(1)}, f32[128,128]{1,0:T(8,128)S(1)}, u32[]{:S(2)}, u32[]{:S(2)}) collective-permute-start(f32[128,128]{1,0:T(8,128)S(1)} %join.1.after.refs_0_), channel_id=1, source_target_pairs={{8,0},{12,4},{0,8},{4,12},{24,16},{28,20},{16,24},{20,28},{9,1},{1... | collective-permute-start | bytes 196616 | tf_op jit(solution)/shard_map/ppermute | solution.py:277
  10.3 4.3 %collective-permute-start.1 = (f32[128,128]{1,0:T(8,128)S(1)}, f32[128,128]{1,0:T(8,128)S(1)}, u32[]{:S(2)}, u32[]{:S(2)}) collective-permute-start(f32[128,128]{1,0:T(8,128)S(1)} %join.1.after.refs_0_), channel_id=1, source_target_pairs={{4,0},{0,4},{12,8},{8,12},{20,16},{16,20},{28,24},{24,28},{5,1},{1... | collective-permute-start | bytes 196616 | tf_op jit(solution)/shard_map/ppermute | solution.py:277
  15.9 3.3 %collective-permute-start.5 = (f32[8,128]{1,0:T(8,128)S(1)}, f32[8,128]{1,0:T(8,128)S(1)}, u32[]{:S(2)}, u32[]{:S(2)}) collective-permute-start(f32[8,128]{1,0:T(8,128)S(1)} %get-tuple-element.20), channel_id=1, source_target_pairs={{0,3},{1,2},{2,1},{3,0},{4,7},{5,6},{6,5},{7,4},{8,11},{9,10},{10,... | collective-permute-start | bytes 12296 | tf_op jit(solution)/shard_map/ppermute | solution.py:284
  15.9 3.7 %collective-permute-start.4 = (f32[8,128]{1,0:T(8,128)S(1)}, f32[8,128]{1,0:T(8,128)S(1)}, u32[]{:S(2)}, u32[]{:S(2)}) collective-permute-start(f32[8,128]{1,0:T(8,128)S(1)} %get-tuple-element.19.after), channel_id=1, source_target_pairs={{0,2},{1,3},{2,0},{3,1},{4,6},{5,7},{6,4},{7,5},{8,10},{9,11},{10,... | collective-permute-start | bytes 12296 | tf_op jit(solution)/shard_map/ppermute | solution.py:284
  18.2 1.4 %collective-permute-start.6 = (f32[8,128]{1,0:T(8,128)S(1)}, f32[8,128]{1,0:T(8,128)S(1)}, u32[]{:S(2)}, u32[]{:S(2)}) collective-permute-start(f32[8,128]{1,0:T(8,128)S(1)} %near.2.after), channel_id=1, source_target_pairs={{0,1},{1,0},{2,3},{3,2},{4,5},{5,4},{6,7},{7,6},{8,9},{9,8},{10,11... | collective-permute-start | bytes 12296 | tf_op jit(solution)/shard_map/ppermute | solution.py:286

commit v3 on v2

--- a/solution.py
+++ b/solution.py
@@ -32,6 +32,11 @@
 def factors(n):
     outer = max(d for d in range(1, n + 1) if n % d == 0 and d * d <= n)
     return outer, n // outer
+
+
+def order(inner):
+    apart = inner // 2
+    return [t for t in range(1, inner) if t != apart] + [apart]
 
 
 def vmem(*xs):
@@ -79,30 +84,34 @@
     )(*vmem(own), *[pltpu.with_memory_space_constraint(x, pltpu.HBM) for x in trains])
 
 
-def join_kernel(*refs):
-    *parts, out = refs
+def join_kernel(count, *refs):
+    out = refs[-1]
+    block = refs[0].shape[0]
+    for i, part in enumerate(refs[:count]):
+        out[pl.ds(i * block, block)] = part[...]
+
+
+def join(parts, *after):
     block = parts[0].shape[0]
-    for i, part in enumerate(parts):
-        out[pl.ds(i * block, block)] = part[...]
-
-
-def join(parts):
-    block = parts[0].shape[0]
-    return pl.pallas_call(
-        join_kernel,
+    return pl.pallas_call(
+        functools.partial(join_kernel, len(parts)),
         out_shape=pltpu.VMEM((len(parts) * block, LANES), jnp.float32),
-        in_specs=[WHOLE] * len(parts),
+        in_specs=[WHOLE] * len(parts) + [ANYWHERE] * len(after),
         out_specs=WHOLE,
         compiler_params=SMALL,
         name="join",
-    )(*vmem(*parts))
+    )(*vmem(*parts, *after))
 
 
 def weigh(outer, inner, width, bites, weight):
     n = outer * inner
     me = lax.axis_index("tok")
     row = lax.broadcasted_iota(jnp.int32, (n, LANES), 0)
-    token = partner(me // inner, row % outer, outer) * inner + partner(me % inner, row // outer, inner)
+    near = row // outer
+    step = jnp.zeros_like(row)
+    for k, t in enumerate(order(inner), 1):
+        step = jnp.where(near == k, t, step)
+    token = partner(me // inner, row % outer, outer) * inner + partner(me % inner, step, inner)
     slots = bites.shape[0] * bites.shape[1]
     count = jnp.zeros((n, LANES), jnp.float32)
     for b in range(bites.shape[0]):
@@ -183,7 +192,7 @@
 
 
 def far_kernel(outer, inner, feat, a_hi, a_lo, g_hi, g_lo, weight, *refs):
-    pieces, (act_pool, grad_pool, *outs), (pool,) = refs[:inner], refs[inner:-1], refs[-1:]
+    pieces, (act_pool, grad_pool, *outs), (pool,) = refs[: inner + 1], refs[inner + 1 : -1], refs[-1:]
     n = outer * inner
     rows, cols = a_hi.shape
     block = pieces[0].shape[0] // outer
@@ -271,10 +280,17 @@
     own = prepare(pool_act.reshape(-1, LANES), pool_grad.reshape(-1, LANES))
 
     own = stage(own, train_act, train_grad)
-    across = [[(partner(i // inner, s, outer) * inner + i % inner, i) for i in range(tok)] for s in range(1, outer)]
-    along = [[(i // inner * inner + partner(i % inner, t, inner), i) for i in range(tok)] for t in range(1, inner)]
-    held = join([own] + [lax.ppermute(own, "tok", pairs) for pairs in across])
-    pieces = [held] + [lax.ppermute(held, "tok", pairs) for pairs in along]
+    *direct, apart = order(inner)
+
+    def exchange(value, s, t):
+        at = [partner(i // inner, s, outer) * inner + partner(i % inner, t, inner) for i in range(tok)]
+        return lax.ppermute(value, "tok", [(source, i) for i, source in enumerate(at)])
+
+    across = [exchange(own, s, 0) for s in range(1, outer)]
+    early = exchange(own, 0, apart)
+    held = join([own, *across])
+    late = join(across, early)
+    pieces = [held] + [exchange(held, 0, t) for t in direct] + [early, exchange(late, 0, apart)]
     parts = split(outer, inner, cols * feat, train_act, train_grad, bites, held)
     act_pool, grad_pool, *sends = far(outer, inner, feat, parts, pieces)
     chips = feat // CORES

time: 20.5 us -> 20 us (0.976)
  waiting for transfers between devices: 4.92 us -> 2.85 us
  starting transfers between devices: 9.5 us -> 11.1 us
    ppermute x4 -> x5, waiting for transfers between devices: 4.58 us -> 2.52 us  [exchange(): lax.ppermute(value, 'tok', [(source, i) for i, source in enumerate(at)])]
    ppermute x4 -> x5, starting transfers between devices: 7.59 us -> 9.17 us  [exchange(): lax.ppermute(value, 'tok', [(source, i) for i, source in enumerate(at)])]
  transfers between devices with their start and end apart: 7 -> 8, of which waited for: 5 -> 3; matrix products, arithmetic and copies ran while one was open for 0% -> 0% of each run, Pallas kernels for 15% -> 15%
where the time goes in v3:
time: 20 us; the launch traced here: 19.7 us
  starting transfers between devices  11.1 us (56%)
  Pallas kernels  5.69 us (28%)
  waiting for transfers between devices  2.85 us (14%)
    ppermute x5, starting transfers between devices, exchange(): lax.ppermute(value, 'tok', [(source, i) for i, source in enumerate(at)])  9.17 us
    ppermute x5, waiting for transfers between devices, exchange(): lax.ppermute(value, 'tok', [(source, i) for i, source in enumerate(at)])  2.52 us
    pallas_call x1, Pallas kernels, split(): pl.pallas_call(functools.partial(split_kernel, outer, inner, width), out_...  1.59 us
    ppermute x2, starting transfers between devices, body(): got.append(lax.ppermute(send, 'feat', pairs))  1.58 us
    pallas_call x2, Pallas kernels, near(): pl.pallas_call(functools.partial(near_kernel, feat, step), out_shape=pltp...  1.43 us
    pallas_call x1, Pallas kernels, far(): pl.pallas_call(functools.partial(far_kernel, outer, inner, feat), out_sha...  1.32 us
    pallas_call x1, Pallas kernels, prepare(): pl.pallas_call(prepare_kernel, out_shape=pltpu.VMEM((2 * act.shape[0], LA...  0.75 us
    pallas_call x1, Pallas kernels, body(): pl.pallas_call(finish_kernel, out_shape=jax.ShapeDtypeStruct((1, rows //...  0.59 us
  transfers between devices with their start and end apart: 8, of which 3 were waited for; matrix products, arithmetic and copies ran while one was open for 0% of the time, Pallas kernels for 15%

profile of v3, /device:TPU:0, one launch (start us, length us, event | category | flops | bytes accessed | tf_op | source)
XLA Modules:
  0.0 19.7 jit_solution(5377129138880978253)
XLA Ops:
  0.0 0.8 %prepare.1.own = f32[64,128]{1,0:T(8,128)S(1)} custom-call(f32[32,128]{1,0:T(8,128)} %bitcast.3, f32[32,128]{1,0:T(8,128)} %bitcast.4), custom_call_target="tpu_custom_call" | custom-call | tf_op jit(solution)/shard_map/prepare/pallas_call | solution.py:61
  0.8 0.0 copy-start
  0.8 0.0 copy-start.1
  0.8 4.1 %collective-permute-start = (f32[64,128]{1,0:T(8,128)S(1)}, f32[64,128]{1,0:T(8,128)S(1)}, u32[]{:S(2)}, u32[]{:S(2)}) collective-permute-start(f32[64,128]{1,0:T(8,128)S(1)} %stage.1.refs_0_), channel_id=1, source_target_pairs={{16,0},{20,4},{24,8},{28,12},{0,16},{4,20},{8,24},{12,28},{17,1},{... | collective-permute-start | bytes 98312 | tf_op jit(solution)/shard_map/ppermute | solution.py:287
  4.9 1.6 %collective-permute-start.3 = (f32[64,128]{1,0:T(8,128)S(1)}, f32[64,128]{1,0:T(8,128)S(1)}, u32[]{:S(2)}, u32[]{:S(2)}) collective-permute-start(f32[64,128]{1,0:T(8,128)S(1)} %stage.1.refs_0_), channel_id=1, source_target_pairs={{8,0},{12,4},{0,8},{4,12},{24,16},{28,20},{16,24},{20,28},{9,1},{1... | collective-permute-start | bytes 98312 | tf_op jit(solution)/shard_map/ppermute | solution.py:287
  6.5 0.8 %collective-permute-done.refs_1_.refs_0_ = f32[64,128]{1,0:T(8,128)S(1)} collective-permute-done((f32[64,128]{1,0:T(8,128)S(1)}, f32[64,128]{1,0:T(8,128)S(1)}, u32[]{:S(2)}, u32[]{:S(2)}) %collective-permute-start) | collective-permute-done | bytes 32800 | tf_op jit(solution)/shard_map/ppermute | solution.py:287
  7.2 2.4 %collective-permute-start.2 = (f32[128,128]{1,0:T(8,128)S(1)}, f32[128,128]{1,0:T(8,128)S(1)}, u32[]{:S(2)}, u32[]{:S(2)}) collective-permute-start(f32[128,128]{1,0:T(8,128)S(1)} %join.2.after.refs_0_), channel_id=1, source_target_pairs={{12,0},{8,4},{4,8},{0,12},{28,16},{24,20},{20,24},{16,28},{13,1},{... | collective-permute-start | bytes 196616 | tf_op jit(solution)/shard_map/ppermute | solution.py:287
  9.6 0.5 %collective-permute-start.1 = (f32[128,128]{1,0:T(8,128)S(1)}, f32[128,128]{1,0:T(8,128)S(1)}, u32[]{:S(2)}, u32[]{:S(2)}) collective-permute-start(f32[128,128]{1,0:T(8,128)S(1)} %join.2.after.refs_0_), channel_id=1, source_target_pairs={{4,0},{0,4},{12,8},{8,12},{20,16},{16,20},{28,24},{24,28},{5,1},{1... | collective-permute-start | bytes 196616 | tf_op jit(solution)/shard_map/ppermute | solution.py:287
  10.2 0.0 collective-permute-done.3.refs_1_.refs_3_
  10.2 0.6 %collective-permute-start.4 = (f32[64,128]{1,0:T(8,128)S(1)}, f32[64,128]{1,0:T(8,128)S(1)}, u32[]{:S(2)}, u32[]{:S(2)}) collective-permute-start(f32[64,128]{1,0:T(8,128)S(1)} %join.3), channel_id=1, source_target_pairs={{8,0},{12,4},{0,8},{4,12},{24,16},{28,20},{16,24},{20,28},{9,1},{1... | collective-permute-start | bytes 98312 | tf_op jit(solution)/shard_map/ppermute | solution.py:287
  10.7 0.0 copy-done
  10.7 0.0 copy-done.1
  10.8 1.6 %split.1 = (bf16[256,4096]{1,0:T(8,128)(2,1)S(1)}, bf16[256,4096]{1,0:T(8,128)(2,1)S(1)}, bf16[256,4096]{1,0:T(8,128)(2,1)S(1)}, bf16[256,4096]{1,0:T(8,128)(2,1)S(1)}, f32[8,128]{1,0:T(8,128)S(1)}) custom-call(f32[256,4096]{1,0:T(8,128)S(1)} %copy-done, f32[256,4096]{1,0:T(8,128)S(1)} %copy-done.1, s32[4,128]{1,0:T(4,128)} %bites.1, ...), custom_call_target="tpu_custom_call" | custom-call | tf_op jit(solution)/shard_map/split/pallas_call | solution.py:142
  12.3 1.7 %collective-permute-done.4.refs_4_ = f32[64,128]{1,0:T(8,128)S(1)} collective-permute-done((f32[64,128]{1,0:T(8,128)S(1)}, f32[64,128]{1,0:T(8,128)S(1)}, u32[]{:S(2)}, u32[]{:S(2)}) %collective-permute-start.4) | collective-permute-done | bytes 32800 | tf_op jit(solution)/shard_map/ppermute | solution.py:287
  14.1 0.0 collective-permute-done.2.refs_2_
  14.1 0.0 collective-permute-done.1.refs_1_
  14.1 1.3 %far.1 = (bf16[16,4096]{1,0:T(8,128)(2,1)S(1)}, bf16[16,4096]{1,0:T(8,128)(2,1)S(1)}, f32[8,128]{1,0:T(8,128)S(1)}, f32[8,128]{1,0:T(8,128)S(1)}) custom-call(bf16[256,4096]{1,0:T(8,128)(2,1)S(1)} %get-tuple-element.14.a_hi, bf16[256,4096]{1,0:T(8,128)(2,1)S(1)} %get-tuple-element.15.a_lo, bf16[256,4096]{1,0:T(8,128)(2,1)S(1)} %get-tuple-element.16.g_hi, ...), custom_call_target="tpu_custom_call" | custom-call | tf_op jit(solution)/shard_map/far/pallas_call | solution.py:225
  15.4 0.0 collective-permute-start.6
  15.4 1.6 %collective-permute-start.5 = (f32[8,128]{1,0:T(8,128)S(1)}, f32[8,128]{1,0:T(8,128)S(1)}, u32[]{:S(2)}, u32[]{:S(2)}) collective-permute-start(f32[8,128]{1,0:T(8,128)S(1)} %get-tuple-element.19.after), channel_id=1, source_target_pairs={{0,2},{1,3},{2,0},{3,1},{4,6},{5,7},{6,4},{7,5},{8,10},{9,11},{10,... | collective-permute-start | bytes 12296 | tf_op jit(solution)/shard_map/ppermute | solution.py:300
  17.0 0.7 %near.2.after = f32[8,128]{1,0:T(8,128)S(1)} custom-call(bf16[256,4096]{1,0:T(8,128)(2,1)S(1)} %get-tuple-element.14.a_hi, bf16[256,4096]{1,0:T(8,128)(2,1)S(1)} %get-tuple-element.15.a_lo, bf16[256,4096]{1,0:T(8,128)(2,1)S(1)} %get-tuple-element.16.g_hi, bf16[256,4096]{1,0:T(8,128)(2,1)S(1)} %get-tuple-element.17.g_lo, ...), custom_call_target="tpu_custom_call" | custom-call | tf_op jit(solution)/shard_map/near/pallas_call | solution.py:238
  17.7 0.3 %collective-permute-start.7 = (f32[8,128]{1,0:T(8,128)S(1)}, f32[8,128]{1,0:T(8,128)S(1)}, u32[]{:S(2)}, u32[]{:S(2)}) collective-permute-start(f32[8,128]{1,0:T(8,128)S(1)} %near.2.after), channel_id=1, source_target_pairs={{0,1},{1,0},{2,3},{3,2},{4,5},{5,4},{6,7},{7,6},{8,9},{9,8},{10,11... | collective-permute-start | bytes 12296 | tf_op jit(solution)/shard_map/ppermute | solution.py:302
  18.0 0.7 %near.3.refs_2_ = f32[8,128]{1,0:T(8,128)S(1)} custom-call(bf16[256,4096]{1,0:T(8,128)(2,1)S(1)} %get-tuple-element.14.a_hi, bf16[256,4096]{1,0:T(8,128)(2,1)S(1)} %get-tuple-element.15.a_lo, bf16[256,4096]{1,0:T(8,128)(2,1)S(1)} %get-tuple-element.16.g_hi, bf16[256,4096]{1,0:T(8,128)(2,1)S(1)} %get-tuple-element.17.g_lo, ...), custom_call_target="tpu_custom_call" | custom-call | tf_op jit(solution)/shard_map/near/pallas_call | solution.py:238
  18.8 0.0 collective-permute-done.6.refs_1_
  18.8 0.3 %collective-permute-done.5.refs_0_ = f32[8,128]{1,0:T(8,128)S(1)} collective-permute-done((f32[8,128]{1,0:T(8,128)S(1)}, f32[8,128]{1,0:T(8,128)S(1)}, u32[]{:S(2)}, u32[]{:S(2)}) %collective-permute-start.5) | collective-permute-done | bytes 4128 | tf_op jit(solution)/shard_map/ppermute | solution.py:300
  19.1 0.0 collective-permute-done.7.refs_1_
  19.1 0.6 %finish.1 = f32[1,64]{1,0:T(1,128)} custom-call(f32[8,128]{1,0:T(8,128)S(1)} %add.1.refs_0_, f32[8,128]{1,0:T(8,128)S(1)} %collective-permute-done.7.refs_1_), custom_call_target="tpu_custom_call" | custom-call | tf_op jit(solution)/shard_map/finish/pallas_call | solution.py:304
  (4 shorter events, 0.0 us)
Async XLA Ops:
  0.8 10.0 %copy-start = (f32[256,4096]{1,0:T(8,128)S(1)}, f32[256,4096]{1,0:T(8,128)}, u32[]{:S(2)}) copy-start(f32[256,4096]{1,0:T(8,128)} %act.1) | copy-start | bytes 12582916
  0.8 10.0 %copy-start.1 = (f32[256,4096]{1,0:T(8,128)S(1)}, f32[256,4096]{1,0:T(8,128)}, u32[]{:S(2)}) copy-start(f32[256,4096]{1,0:T(8,128)} %grad.1) | copy-start | bytes 12582916
  0.8 6.4 %collective-permute-start = (f32[64,128]{1,0:T(8,128)S(1)}, f32[64,128]{1,0:T(8,128)S(1)}, u32[]{:S(2)}, u32[]{:S(2)}) collective-permute-start(f32[64,128]{1,0:T(8,128)S(1)} %stage.1.refs_0_), channel_id=1, source_target_pairs={{16,0},{20,4},{24,8},{28,12},{0,16},{4,20},{8,24},{12,28},{17,1},{... | collective-permute-start | bytes 98312 | tf_op jit(solution)/shard_map/ppermute | solution.py:287
  4.9 5.3 %collective-permute-start.3 = (f32[64,128]{1,0:T(8,128)S(1)}, f32[64,128]{1,0:T(8,128)S(1)}, u32[]{:S(2)}, u32[]{:S(2)}) collective-permute-start(f32[64,128]{1,0:T(8,128)S(1)} %stage.1.refs_0_), channel_id=1, source_target_pairs={{8,0},{12,4},{0,8},{4,12},{24,16},{28,20},{16,24},{20,28},{9,1},{1... | collective-permute-start | bytes 98312 | tf_op jit(solution)/shard_map/ppermute | solution.py:287
  7.2 6.8 %collective-permute-start.2 = (f32[128,128]{1,0:T(8,128)S(1)}, f32[128,128]{1,0:T(8,128)S(1)}, u32[]{:S(2)}, u32[]{:S(2)}) collective-permute-start(f32[128,128]{1,0:T(8,128)S(1)} %join.2.after.refs_0_), channel_id=1, source_target_pairs={{12,0},{8,4},{4,8},{0,12},{28,16},{24,20},{20,24},{16,28},{13,1},{... | collective-permute-start | bytes 196616 | tf_op jit(solution)/shard_map/ppermute | solution.py:287
  9.6 4.5 %collective-permute-start.1 = (f32[128,128]{1,0:T(8,128)S(1)}, f32[128,128]{1,0:T(8,128)S(1)}, u32[]{:S(2)}, u32[]{:S(2)}) collective-permute-start(f32[128,128]{1,0:T(8,128)S(1)} %join.2.after.refs_0_), channel_id=1, source_target_pairs={{4,0},{0,4},{12,8},{8,12},{20,16},{16,20},{28,24},{24,28},{5,1},{1... | collective-permute-start | bytes 196616 | tf_op jit(solution)/shard_map/ppermute | solution.py:287
  10.2 3.9 %collective-permute-start.4 = (f32[64,128]{1,0:T(8,128)S(1)}, f32[64,128]{1,0:T(8,128)S(1)}, u32[]{:S(2)}, u32[]{:S(2)}) collective-permute-start(f32[64,128]{1,0:T(8,128)S(1)} %join.3), channel_id=1, source_target_pairs={{8,0},{12,4},{0,8},{4,12},{24,16},{28,20},{16,24},{20,28},{9,1},{1... | collective-permute-start | bytes 98312 | tf_op jit(solution)/shard_map/ppermute | solution.py:287
  15.4 3.3 %collective-permute-start.6 = (f32[8,128]{1,0:T(8,128)S(1)}, f32[8,128]{1,0:T(8,128)S(1)}, u32[]{:S(2)}, u32[]{:S(2)}) collective-permute-start(f32[8,128]{1,0:T(8,128)S(1)} %get-tuple-element.20), channel_id=1, source_target_pairs={{0,3},{1,2},{2,1},{3,0},{4,7},{5,6},{6,5},{7,4},{8,11},{9,10},{10,... | collective-permute-start | bytes 12296 | tf_op jit(solution)/shard_map/ppermute | solution.py:300
  15.4 3.7 %collective-permute-start.5 = (f32[8,128]{1,0:T(8,128)S(1)}, f32[8,128]{1,0:T(8,128)S(1)}, u32[]{:S(2)}, u32[]{:S(2)}) collective-permute-start(f32[8,128]{1,0:T(8,128)S(1)} %get-tuple-element.19.after), channel_id=1, source_target_pairs={{0,2},{1,3},{2,0},{3,1},{4,6},{5,7},{6,4},{7,5},{8,10},{9,11},{10,... | collective-permute-start | bytes 12296 | tf_op jit(solution)/shard_map/ppermute | solution.py:300
  17.7 1.4 %collective-permute-start.7 = (f32[8,128]{1,0:T(8,128)S(1)}, f32[8,128]{1,0:T(8,128)S(1)}, u32[]{:S(2)}, u32[]{:S(2)}) collective-permute-start(f32[8,128]{1,0:T(8,128)S(1)} %near.2.after), channel_id=1, source_target_pairs={{0,1},{1,0},{2,3},{3,2},{4,5},{5,4},{6,7},{7,6},{8,9},{9,8},{10,11... | collective-permute-start | bytes 12296 | tf_op jit(solution)/shard_map/ppermute | solution.py:302

commit v4 on v3

--- a/solution.py
+++ b/solution.py
@@ -121,29 +121,31 @@
     weight[...] = jnp.broadcast_to(total * (1.0 / (width * slots**0.5)), (n, LANES))
 
 
-def split_rows(train, hi, lo):
+def split_rows(train, wide):
+    cols = train.shape[1]
+
     @pl.loop(0, train.shape[0] // 16)
     def _(r):
         span = pl.ds(pl.multiple_of(r * 16, 16), 16)
-        hi[span], lo[span] = halves(train[span])
-
-
-def split_kernel(outer, inner, width, act, grad, bites, after, a_hi, a_lo, g_hi, g_lo, weight, index, sem):
+        wide[span, :cols], wide[span, cols:] = halves(train[span])
+
+
+def split_kernel(outer, inner, width, act, grad, bites, after, act_wide, grad_wide, weight, index, sem):
     copy = pltpu.make_async_copy(bites, index, sem)
     copy.start()
-    split_rows(act, a_hi, a_lo)
-    split_rows(grad, g_hi, g_lo)
+    split_rows(act, act_wide)
+    split_rows(grad, grad_wide)
     copy.wait()
     weigh(outer, inner, width, index, weight)
 
 
 def split(outer, inner, width, act, grad, bites, after):
-    half = pltpu.VMEM(act.shape, jnp.bfloat16)
+    wide = pltpu.VMEM((act.shape[0], 2 * act.shape[1]), jnp.bfloat16)
     return pl.pallas_call(
         functools.partial(split_kernel, outer, inner, width),
-        out_shape=[half] * 4 + [pltpu.VMEM((outer * inner, LANES), jnp.float32)],
+        out_shape=[wide] * 2 + [pltpu.VMEM((outer * inner, LANES), jnp.float32)],
         in_specs=[WHOLE, WHOLE, ANYWHERE, ANYWHERE],
-        out_specs=[WHOLE] * 5,
+        out_specs=[WHOLE] * 3,
         scratch_shapes=[pltpu.VMEM(bites.shape, jnp.int32), pltpu.SemaphoreType.DMA],
         compiler_params=SMALL,
         name="split",
@@ -159,27 +161,26 @@
     return jnp.concatenate([jnp.concatenate(tops, axis=1), jnp.concatenate(bottoms, axis=1)], axis=0)
 
 
-def product(both, hi, lo, start, rows):
+def product(both, wide, start, rows):
     n = both.shape[0] // 2
     dims = (((1,), (1,)), ((), ()))
     span = pl.ds(pl.multiple_of(start, 32), rows)
-    one = lax.dot_general(both, hi[span], dims, preferred_element_type=jnp.float32)
-    two = lax.dot_general(both[:n], lo[span], dims, preferred_element_type=jnp.float32)
-    return one[:n] + one[n:] + two
+    out = lax.dot_general(jnp.concatenate([both, both], axis=1), wide[span], dims, preferred_element_type=jnp.float32)
+    return out[:n] + out[n:]
 
 
 def device_grams(act_pool, grad_pool, parts, weight, to, share):
-    a_hi, a_lo, g_hi, g_lo = parts
-    act = product(act_pool[...], a_hi, a_lo, to * share, share) * weight[:, :share]
-    grad = product(grad_pool[...], g_hi, g_lo, to * share, share)
+    act_wide, grad_wide = parts
+    act = product(act_pool[...], act_wide, to * share, share) * weight[:, :share]
+    grad = product(grad_pool[...], grad_wide, to * share, share)
     return jnp.concatenate([act, grad], axis=1)
 
 
 def chip_grams(act_pool, grad_pool, parts, weight, chip, share):
-    a_hi, a_lo, g_hi, g_lo = parts
+    act_wide, grad_wide = parts
     rows = CORES * share
-    act = product(act_pool[...], a_hi, a_lo, chip * rows, rows) * weight[:, :rows]
-    grad = product(grad_pool[...], g_hi, g_lo, chip * rows, rows)
+    act = product(act_pool[...], act_wide, chip * rows, rows) * weight[:, :rows]
+    grad = product(grad_pool[...], grad_wide, chip * rows, rows)
     return [
         jnp.concatenate([act[:, c * share : (c + 1) * share], grad[:, c * share : (c + 1) * share]], axis=1)
         for c in range(CORES)
@@ -191,10 +192,10 @@
     other[...] = jnp.where(me % CORES == 0, pieces[1], pieces[0])
 
 
-def far_kernel(outer, inner, feat, a_hi, a_lo, g_hi, g_lo, weight, *refs):
+def far_kernel(outer, inner, feat, act_wide, grad_wide, weight, *refs):
     pieces, (act_pool, grad_pool, *outs), (pool,) = refs[: inner + 1], refs[inner + 1 : -1], refs[-1:]
     n = outer * inner
-    rows, cols = a_hi.shape
+    rows, cols = act_wide.shape[0], act_pool.shape[1]
     block = pieces[0].shape[0] // outer
     start = 0
     for piece in pieces:
@@ -206,19 +207,19 @@
     chips = feat // CORES
     for s in range(1, chips):
         to = partner_to(me // CORES, s, chips)
-        got = chip_grams(act_pool, grad_pool, (a_hi, a_lo, g_hi, g_lo), weight, to, rows // feat)
+        got = chip_grams(act_pool, grad_pool, (act_wide, grad_wide), weight, to, rows // feat)
         swap(got, me, outs[CORES * (s - 1)], outs[CORES * (s - 1) + 1])
 
 
-def near_kernel(feat, step, a_hi, a_lo, g_hi, g_lo, weight, act_pool, grad_pool, after, out):
+def near_kernel(feat, step, act_wide, grad_wide, weight, act_pool, grad_pool, after, out):
     me = lax.axis_index("feat")
     to = me // CORES * CORES + (me + step) % CORES
-    out[...] = device_grams(act_pool, grad_pool, (a_hi, a_lo, g_hi, g_lo), weight, to, a_hi.shape[0] // feat)
+    out[...] = device_grams(act_pool, grad_pool, (act_wide, grad_wide), weight, to, act_wide.shape[0] // feat)
 
 
 def far(outer, inner, feat, parts, pieces):
     n = outer * inner
-    rows, cols = parts[0].shape
+    rows, cols = parts[0].shape[0], parts[0].shape[1] // 2
     args = vmem(*parts, *pieces)
     piece = pltpu.VMEM((n, 2 * rows // feat), jnp.float32)
     outs = [pltpu.VMEM((2 * n, cols), jnp.bfloat16)] * 2 + [piece] * (feat - CORES)

time: 20 us -> 20 us (level)
  no operation moved by 1% of the time
where the time goes in v4:
time: 20 us; the launch traced here: 19.7 us
  starting transfers between devices  11.1 us (56%)
  Pallas kernels  5.69 us (28%)
  waiting for transfers between devices  2.83 us (14%)
    ppermute x5, starting transfers between devices, exchange(): lax.ppermute(value, 'tok', [(source, i) for i, source in enumerate(at)])  9.17 us
    ppermute x5, waiting for transfers between devices, exchange(): lax.ppermute(value, 'tok', [(source, i) for i, source in enumerate(at)])  2.49 us
    pallas_call x1, Pallas kernels, split(): pl.pallas_call(functools.partial(split_kernel, outer, inner, width), out_...  1.61 us
    ppermute x2, starting transfers between devices, body(): got.append(lax.ppermute(send, 'feat', pairs))  1.57 us
    pallas_call x2, Pallas kernels, near(): pl.pallas_call(functools.partial(near_kernel, feat, step), out_shape=pltp...  1.43 us
    pallas_call x1, Pallas kernels, far(): pl.pallas_call(functools.partial(far_kernel, outer, inner, feat), out_sha...  1.3 us
    pallas_call x1, Pallas kernels, prepare(): pl.pallas_call(prepare_kernel, out_shape=pltpu.VMEM((2 * act.shape[0], LA...  0.75 us
    pallas_call x1, Pallas kernels, body(): pl.pallas_call(finish_kernel, out_shape=jax.ShapeDtypeStruct((1, rows //...  0.59 us
  transfers between devices with their start and end apart: 8, of which 3 were waited for; matrix products, arithmetic and copies ran while one was open for 0% of the time, Pallas kernels for 15%

profile of v4, /device:TPU:0, one launch (start us, length us, event | category | flops | bytes accessed | tf_op | source)
XLA Modules:
  0.0 19.7 jit_solution(7936100179554504711)
XLA Ops:
  0.0 0.8 %prepare.1.own = f32[64,128]{1,0:T(8,128)S(1)} custom-call(f32[32,128]{1,0:T(8,128)} %bitcast.3, f32[32,128]{1,0:T(8,128)} %bitcast.4), custom_call_target="tpu_custom_call" | custom-call | tf_op jit(solution)/shard_map/prepare/pallas_call | solution.py:61
  0.8 0.0 copy-start
  0.8 0.0 copy-start.1
  0.8 4.1 %collective-permute-start = (f32[64,128]{1,0:T(8,128)S(1)}, f32[64,128]{1,0:T(8,128)S(1)}, u32[]{:S(2)}, u32[]{:S(2)}) collective-permute-start(f32[64,128]{1,0:T(8,128)S(1)} %stage.1.refs_0_), channel_id=1, source_target_pairs={{16,0},{20,4},{24,8},{28,12},{0,16},{4,20},{8,24},{12,28},{17,1},{... | collective-permute-start | bytes 98312 | tf_op jit(solution)/shard_map/ppermute | solution.py:288
  4.9 1.6 %collective-permute-start.3 = (f32[64,128]{1,0:T(8,128)S(1)}, f32[64,128]{1,0:T(8,128)S(1)}, u32[]{:S(2)}, u32[]{:S(2)}) collective-permute-start(f32[64,128]{1,0:T(8,128)S(1)} %stage.1.refs_0_), channel_id=1, source_target_pairs={{8,0},{12,4},{0,8},{4,12},{24,16},{28,20},{16,24},{20,28},{9,1},{1... | collective-permute-start | bytes 98312 | tf_op jit(solution)/shard_map/ppermute | solution.py:288
  6.5 0.8 %collective-permute-done.refs_1_.refs_0_ = f32[64,128]{1,0:T(8,128)S(1)} collective-permute-done((f32[64,128]{1,0:T(8,128)S(1)}, f32[64,128]{1,0:T(8,128)S(1)}, u32[]{:S(2)}, u32[]{:S(2)}) %collective-permute-start) | collective-permute-done | bytes 32800 | tf_op jit(solution)/shard_map/ppermute | solution.py:288
  7.2 2.4 %collective-permute-start.2 = (f32[128,128]{1,0:T(8,128)S(1)}, f32[128,128]{1,0:T(8,128)S(1)}, u32[]{:S(2)}, u32[]{:S(2)}) collective-permute-start(f32[128,128]{1,0:T(8,128)S(1)} %join.2.after.refs_0_), channel_id=1, source_target_pairs={{12,0},{8,4},{4,8},{0,12},{28,16},{24,20},{20,24},{16,28},{13,1},{... | collective-permute-start | bytes 196616 | tf_op jit(solution)/shard_map/ppermute | solution.py:288
  9.6 0.5 %collective-permute-start.1 = (f32[128,128]{1,0:T(8,128)S(1)}, f32[128,128]{1,0:T(8,128)S(1)}, u32[]{:S(2)}, u32[]{:S(2)}) collective-permute-start(f32[128,128]{1,0:T(8,128)S(1)} %join.2.after.refs_0_), channel_id=1, source_target_pairs={{4,0},{0,4},{12,8},{8,12},{20,16},{16,20},{28,24},{24,28},{5,1},{1... | collective-permute-start | bytes 196616 | tf_op jit(solution)/shard_map/ppermute | solution.py:288
  10.2 0.0 collective-permute-done.3.refs_1_.refs_3_
  10.2 0.6 %collective-permute-start.4 = (f32[64,128]{1,0:T(8,128)S(1)}, f32[64,128]{1,0:T(8,128)S(1)}, u32[]{:S(2)}, u32[]{:S(2)}) collective-permute-start(f32[64,128]{1,0:T(8,128)S(1)} %join.3), channel_id=1, source_target_pairs={{8,0},{12,4},{0,8},{4,12},{24,16},{28,20},{16,24},{20,28},{9,1},{1... | collective-permute-start | bytes 98312 | tf_op jit(solution)/shard_map/ppermute | solution.py:288
  10.7 0.0 copy-done
  10.7 0.0 copy-done.1
  10.8 1.6 %split.1 = (bf16[256,8192]{1,0:T(8,128)(2,1)S(1)}, bf16[256,8192]{1,0:T(8,128)(2,1)S(1)}, f32[8,128]{1,0:T(8,128)S(1)}) custom-call(f32[256,4096]{1,0:T(8,128)S(1)} %copy-done, f32[256,4096]{1,0:T(8,128)S(1)} %copy-done.1, s32[4,128]{1,0:T(4,128)} %bites.1, f32[128,128]{1,0:T(8,128)S(1)} %join.2.after.refs_0_), custom_call_target="tpu_custom_call" | custom-call | tf_op jit(solution)/shard_map/split/pallas_call | solution.py:144
  12.4 1.7 %collective-permute-done.4.refs_4_ = f32[64,128]{1,0:T(8,128)S(1)} collective-permute-done((f32[64,128]{1,0:T(8,128)S(1)}, f32[64,128]{1,0:T(8,128)S(1)}, u32[]{:S(2)}, u32[]{:S(2)}) %collective-permute-start.4) | collective-permute-done | bytes 32800 | tf_op jit(solution)/shard_map/ppermute | solution.py:288
  14.1 0.0 collective-permute-done.2.refs_2_
  14.1 0.0 collective-permute-done.1.refs_1_
  14.1 1.3 %far.1 = (bf16[16,4096]{1,0:T(8,128)(2,1)S(1)}, bf16[16,4096]{1,0:T(8,128)(2,1)S(1)}, f32[8,128]{1,0:T(8,128)S(1)}, f32[8,128]{1,0:T(8,128)S(1)}) custom-call(bf16[256,8192]{1,0:T(8,128)(2,1)S(1)} %get-tuple-element.12.act_wide, bf16[256,8192]{1,0:T(8,128)(2,1)S(1)} %get-tuple-element.13.grad_wide, f32[8,128]{1,0:T(8,128)S(1)} %get-tuple-element.14.weight, ...), custom_call_target="tpu_custom_call" | custom-call | tf_op jit(solution)/shard_map/far/pallas_call | solution.py:226
  15.4 0.0 collective-permute-start.6
  15.4 1.6 %collective-permute-start.5 = (f32[8,128]{1,0:T(8,128)S(1)}, f32[8,128]{1,0:T(8,128)S(1)}, u32[]{:S(2)}, u32[]{:S(2)}) collective-permute-start(f32[8,128]{1,0:T(8,128)S(1)} %get-tuple-element.15.after), channel_id=1, source_target_pairs={{0,2},{1,3},{2,0},{3,1},{4,6},{5,7},{6,4},{7,5},{8,10},{9,11},{10,... | collective-permute-start | bytes 12296 | tf_op jit(solution)/shard_map/ppermute | solution.py:301
  17.0 0.7 %near.2.after = f32[8,128]{1,0:T(8,128)S(1)} custom-call(bf16[256,8192]{1,0:T(8,128)(2,1)S(1)} %get-tuple-element.12.act_wide, bf16[256,8192]{1,0:T(8,128)(2,1)S(1)} %get-tuple-element.13.grad_wide, f32[8,128]{1,0:T(8,128)S(1)} %get-tuple-element.14.weight, bf16[16,4096]{1,0:T(8,128)(2,1)S(1)} %get-tuple-element.17.act_pool, ...), custom_call_target="tpu_custom_call" | custom-call | tf_op jit(solution)/shard_map/near/pallas_call | solution.py:239
  17.7 0.3 %collective-permute-start.7 = (f32[8,128]{1,0:T(8,128)S(1)}, f32[8,128]{1,0:T(8,128)S(1)}, u32[]{:S(2)}, u32[]{:S(2)}) collective-permute-start(f32[8,128]{1,0:T(8,128)S(1)} %near.2.after), channel_id=1, source_target_pairs={{0,1},{1,0},{2,3},{3,2},{4,5},{5,4},{6,7},{7,6},{8,9},{9,8},{10,11... | collective-permute-start | bytes 12296 | tf_op jit(solution)/shard_map/ppermute | solution.py:303
  18.0 0.7 %near.3.refs_2_ = f32[8,128]{1,0:T(8,128)S(1)} custom-call(bf16[256,8192]{1,0:T(8,128)(2,1)S(1)} %get-tuple-element.12.act_wide, bf16[256,8192]{1,0:T(8,128)(2,1)S(1)} %get-tuple-element.13.grad_wide, f32[8,128]{1,0:T(8,128)S(1)} %get-tuple-element.14.weight, bf16[16,4096]{1,0:T(8,128)(2,1)S(1)} %get-tuple-element.17.act_pool, ...), custom_call_target="tpu_custom_call" | custom-call | tf_op jit(solution)/shard_map/near/pallas_call | solution.py:239
  18.7 0.0 collective-permute-done.6.refs_1_
  18.7 0.3 %collective-permute-done.5.refs_0_ = f32[8,128]{1,0:T(8,128)S(1)} collective-permute-done((f32[8,128]{1,0:T(8,128)S(1)}, f32[8,128]{1,0:T(8,128)S(1)}, u32[]{:S(2)}, u32[]{:S(2)}) %collective-permute-start.5) | collective-permute-done | bytes 4128 | tf_op jit(solution)/shard_map/ppermute | solution.py:301
  19.1 0.0 collective-permute-done.7.refs_1_
  19.1 0.6 %finish.1 = f32[1,64]{1,0:T(1,128)} custom-call(f32[8,128]{1,0:T(8,128)S(1)} %add.1.refs_0_, f32[8,128]{1,0:T(8,128)S(1)} %collective-permute-done.7.refs_1_), custom_call_target="tpu_custom_call" | custom-call | tf_op jit(solution)/shard_map/finish/pallas_call | solution.py:305
  (4 shorter events, 0.0 us)
Async XLA Ops:
  0.8 10.0 %copy-start = (f32[256,4096]{1,0:T(8,128)S(1)}, f32[256,4096]{1,0:T(8,128)}, u32[]{:S(2)}) copy-start(f32[256,4096]{1,0:T(8,128)} %act.1) | copy-start | bytes 12582916
  0.8 10.0 %copy-start.1 = (f32[256,4096]{1,0:T(8,128)S(1)}, f32[256,4096]{1,0:T(8,128)}, u32[]{:S(2)}) copy-start(f32[256,4096]{1,0:T(8,128)} %grad.1) | copy-start | bytes 12582916
  0.8 6.4 %collective-permute-start = (f32[64,128]{1,0:T(8,128)S(1)}, f32[64,128]{1,0:T(8,128)S(1)}, u32[]{:S(2)}, u32[]{:S(2)}) collective-permute-start(f32[64,128]{1,0:T(8,128)S(1)} %stage.1.refs_0_), channel_id=1, source_target_pairs={{16,0},{20,4},{24,8},{28,12},{0,16},{4,20},{8,24},{12,28},{17,1},{... | collective-permute-start | bytes 98312 | tf_op jit(solution)/shard_map/ppermute | solution.py:288
  4.9 5.3 %collective-permute-start.3 = (f32[64,128]{1,0:T(8,128)S(1)}, f32[64,128]{1,0:T(8,128)S(1)}, u32[]{:S(2)}, u32[]{:S(2)}) collective-permute-start(f32[64,128]{1,0:T(8,128)S(1)} %stage.1.refs_0_), channel_id=1, source_target_pairs={{8,0},{12,4},{0,8},{4,12},{24,16},{28,20},{16,24},{20,28},{9,1},{1... | collective-permute-start | bytes 98312 | tf_op jit(solution)/shard_map/ppermute | solution.py:288
  7.2 6.8 %collective-permute-start.2 = (f32[128,128]{1,0:T(8,128)S(1)}, f32[128,128]{1,0:T(8,128)S(1)}, u32[]{:S(2)}, u32[]{:S(2)}) collective-permute-start(f32[128,128]{1,0:T(8,128)S(1)} %join.2.after.refs_0_), channel_id=1, source_target_pairs={{12,0},{8,4},{4,8},{0,12},{28,16},{24,20},{20,24},{16,28},{13,1},{... | collective-permute-start | bytes 196616 | tf_op jit(solution)/shard_map/ppermute | solution.py:288
  9.6 4.5 %collective-permute-start.1 = (f32[128,128]{1,0:T(8,128)S(1)}, f32[128,128]{1,0:T(8,128)S(1)}, u32[]{:S(2)}, u32[]{:S(2)}) collective-permute-start(f32[128,128]{1,0:T(8,128)S(1)} %join.2.after.refs_0_), channel_id=1, source_target_pairs={{4,0},{0,4},{12,8},{8,12},{20,16},{16,20},{28,24},{24,28},{5,1},{1... | collective-permute-start | bytes 196616 | tf_op jit(solution)/shard_map/ppermute | solution.py:288
  10.2 3.9 %collective-permute-start.4 = (f32[64,128]{1,0:T(8,128)S(1)}, f32[64,128]{1,0:T(8,128)S(1)}, u32[]{:S(2)}, u32[]{:S(2)}) collective-permute-start(f32[64,128]{1,0:T(8,128)S(1)} %join.3), channel_id=1, source_target_pairs={{8,0},{12,4},{0,8},{4,12},{24,16},{28,20},{16,24},{20,28},{9,1},{1... | collective-permute-start | bytes 98312 | tf_op jit(solution)/shard_map/ppermute | solution.py:288
  15.4 3.3 %collective-permute-start.6 = (f32[8,128]{1,0:T(8,128)S(1)}, f32[8,128]{1,0:T(8,128)S(1)}, u32[]{:S(2)}, u32[]{:S(2)}) collective-permute-start(f32[8,128]{1,0:T(8,128)S(1)} %get-tuple-element.16), channel_id=1, source_target_pairs={{0,3},{1,2},{2,1},{3,0},{4,7},{5,6},{6,5},{7,4},{8,11},{9,10},{10,... | collective-permute-start | bytes 12296 | tf_op jit(solution)/shard_map/ppermute | solution.py:301
  15.4 3.7 %collective-permute-start.5 = (f32[8,128]{1,0:T(8,128)S(1)}, f32[8,128]{1,0:T(8,128)S(1)}, u32[]{:S(2)}, u32[]{:S(2)}) collective-permute-start(f32[8,128]{1,0:T(8,128)S(1)} %get-tuple-element.15.after), channel_id=1, source_target_pairs={{0,2},{1,3},{2,0},{3,1},{4,6},{5,7},{6,4},{7,5},{8,10},{9,11},{10,... | collective-permute-start | bytes 12296 | tf_op jit(solution)/shard_map/ppermute | solution.py:301
  17.7 1.4 %collective-permute-start.7 = (f32[8,128]{1,0:T(8,128)S(1)}, f32[8,128]{1,0:T(8,128)S(1)}, u32[]{:S(2)}, u32[]{:S(2)}) collective-permute-start(f32[8,128]{1,0:T(8,128)S(1)} %near.2.after), channel_id=1, source_target_pairs={{0,1},{1,0},{2,3},{3,2},{4,5},{5,4},{6,7},{7,6},{8,9},{9,8},{10,11... | collective-permute-start | bytes 12296 | tf_op jit(solution)/shard_map/ppermute | solution.py:303
